TPU v7x, 32 devices: a whole 2x2x4 slice. The times are simulated.
32 devices in a mesh: grp: 2 (over y), pool: 4 (over z), head: 2 (over x), sub: 2 (over core).
Axes of the slice: x: 2, y: 2, z: 4, core: 2. Of those that a mesh axis runs over, the one named last changes fastest.
Arguments:
- pool: bfloat16 [192, 64, 576], P(('grp', 'pool')), parts along dimension 0, may hold values from -100 to 100
- block_table: int32 [16, 32], P(('grp', 'pool')), parts along dimension 0, may hold values from 0 to 95, as said below
- lengths: int32 [16], P(('grp', 'pool')), parts along dimension 0, may hold values from 1 to 2047, as said below
- new_slot: int32 [16], P(('grp', 'pool')), parts along dimension 0, may hold values from 0 to 7, each once
- q_nope: bfloat16 [16, 128, 128], P(('grp', 'pool'), ('head', 'sub')), parts along dimension 0, may hold values from -6 to 6
- q_rope: bfloat16 [16, 128, 64], P(('grp', 'pool'), ('head', 'sub')), parts along dimension 0, may hold values from -6 to 6
- new_latent: bfloat16 [16, 576], P(('grp', 'pool')), parts along dimension 0, may hold values from -700 to 700
- kv_gain: bfloat16 [512], replicated, may hold values from 0.5 to 1.5
- w_uk: bfloat16 [128, 128, 512], P(('head', 'sub')), may hold values from -0.5 to 0.5
- w_uv: bfloat16 [128, 512, 128], P(('head', 'sub')), may hold values from -0.25 to 0.25
Outputs:
- attn_out: bfloat16 [16, 128, 128], P(('grp', 'pool'), ('head', 'sub')), parts along dimension 0
- new_blocks: bfloat16 [16, 64, 576], P(('grp', 'pool'), ('head', 'sub')), parts along dimension 0
There are 2 independent parts, one for each index of `grp`. A program takes and returns all parts, laid end to end along the dimension named above; an argument that names none is the same for every part. Nothing has to cross between parts.
Inputs may be any that keep to these rules, and one draw needn't show every extreme that they name: block_table[r, j] = o * 24 + s names slot s of owner o, where o = (block_table[r, 0] // 24 + j) mod 4 for every j; the blocks that hold positions below lengths[r] are distinct over all rows; entries for j at or beyond (lengths[r] + 63) // 64 are placeholders. `lengths`: exactly one row of a part has 2047. new_slot[r] = o * 2 + s returns row r's block to slot s of owner o; each value once.
All inputs are finite; a program needn't handle non-finite values.
Results may differ from a plain program's by a relative error of at most 0.0075.
Values may be sent and summed in bfloat16 or wider, within the bound.
No kernel may reach another device: no remote copies, remote signals or barrier semaphores. Data moves between devices by JAX's collectives and lax.ppermute only.
A program may use at most 64 MiB of HBM per device.

v0:
```python
import jax
import jax.numpy as jnp
from jax import lax
from jax.sharding import PartitionSpec as P

EPS = 1e-06
SCALE = 192.0 ** (-0.5)


def rotate(values, positions):
    half_width = values.shape[-1] // 2
    frequency = 10000.0 ** (-jnp.arange(half_width, dtype=jnp.float32) / half_width)
    angles = positions.astype(jnp.float32)[..., None] * frequency
    cosine = jnp.cos(angles)
    sine_part = jnp.sin(angles)
    first_half = values[..., :half_width]
    second_half = values[..., half_width:]
    return jnp.concatenate(
        [
            first_half * cosine - second_half * sine_part,
            second_half * cosine + first_half * sine_part,
        ],
        axis=-1,
    )


def per_device(
    pool, block_table, lengths, new_slot, q_nope, q_rope, new_latent, kv_gain, w_uk, w_uv
):
    owners = lax.axis_size("pool")
    groups = lax.axis_size(("head", "sub"))
    part_index = lax.axis_index(("head", "sub"))
    slot_count, block_len, lat_width = pool.shape
    row_dev, maxblk = block_table.shape
    latent_width = kv_gain.shape[0]
    row_count = row_dev * owners
    per_owner = maxblk // owners
    token_span = block_len // groups
    latent_raw = new_latent[:, :latent_width].astype(jnp.float32)
    mean_square = jnp.mean(latent_raw * latent_raw, axis=-1, keepdims=True)
    new_cache_lat = (
        latent_raw * lax.rsqrt(mean_square + EPS) * kv_gain.astype(jnp.float32)
    ).astype(jnp.bfloat16)
    new_key = rotate(new_latent[:, latent_width:].astype(jnp.float32), lengths)
    query_rot = rotate(q_rope.astype(jnp.float32), lengths[:, None])
    new_vector = jnp.concatenate([new_cache_lat, new_key.astype(jnp.bfloat16)], axis=1)
    query_lat = jnp.einsum("rhn,hnl->rhl", q_nope, w_uk, preferred_element_type=jnp.float32).astype(
        jnp.bfloat16
    )
    new_score = jnp.einsum(
        "rhl,rl->rh", query_lat, new_cache_lat, preferred_element_type=jnp.float32
    )
    new_score = SCALE * (
        new_score + jnp.einsum("rhe,re->rh", query_rot, new_key, precision=lax.Precision.HIGHEST)
    )
    token_ids = part_index * token_span + jnp.arange(token_span, dtype=jnp.int32)
    first_owner = block_table[:, 0] // slot_count
    owner_ids = jnp.arange(owners, dtype=jnp.int32)
    step_ids = jnp.arange(per_owner, dtype=jnp.int32)
    block_ids = (
        owner_ids[:, None, None] - first_owner[None, :, None]
    ) % owners + owners * step_ids[None, None, :]
    wanted = jnp.take_along_axis(
        jnp.broadcast_to(block_table[None], (owners, row_dev, maxblk)), block_ids, axis=2
    )
    requested = lax.all_to_all(wanted % slot_count, "pool", split_axis=0, concat_axis=0, tiled=True)
    outgoing = pool[requested]
    fetched = lax.all_to_all(outgoing, "pool", split_axis=0, concat_axis=0, tiled=True)
    positions = block_len * block_ids[..., None] + jnp.arange(block_len, dtype=jnp.int32)
    is_valid = jnp.transpose(positions < lengths[None, :, None, None], (1, 0, 2, 3))[:, None]
    scores = jnp.einsum(
        "oktil,khl->khoti",
        fetched[..., :latent_width],
        query_lat,
        preferred_element_type=jnp.float32,
    )
    scores = scores + jnp.einsum(
        "oktie,khe->khoti",
        fetched[..., latent_width:],
        query_rot,
        precision=lax.Precision.HIGHEST,
        preferred_element_type=jnp.float32,
    )
    scores = SCALE * scores
    group_max = jnp.max(jnp.where(is_valid, scores, -1e30), axis=(3, 4))
    row_max = jnp.maximum(jnp.max(group_max, axis=2), new_score)
    weights = jnp.where(is_valid, jnp.exp(scores - group_max[..., None, None]), 0.0).astype(
        jnp.bfloat16
    )
    factor = jnp.exp(group_max - row_max[..., None])
    group_total = jnp.sum(weights.astype(jnp.float32), axis=(3, 4))
    group_weighted = jnp.einsum(
        "khoti,oktil->khol",
        weights,
        fetched[..., :latent_width],
        preferred_element_type=jnp.float32,
    )
    new_weight = jnp.exp(new_score - row_max).astype(jnp.bfloat16)
    denominator = jnp.sum(group_total * factor, axis=2) + new_weight.astype(jnp.float32)
    weighted = jnp.einsum("khol,kho->khl", group_weighted, factor, precision=lax.Precision.HIGHEST)
    weighted = (
        weighted
        + new_weight.astype(jnp.float32)[..., None] * new_cache_lat.astype(jnp.float32)[:, None, :]
    )
    tail_index = lengths // block_len
    tail_holder = (first_owner + tail_index) % owners
    tail_step = tail_index // owners
    tail_rows = fetched[tail_holder, jnp.arange(row_dev), tail_step]
    tail_rows = lax.dynamic_slice_in_dim(tail_rows, part_index * token_span, token_span, 1)
    tail_pos = block_len * tail_index[:, None] + token_ids[None, :]
    term_rows = jnp.where(
        (tail_pos < lengths[:, None])[..., None], tail_rows, jnp.zeros_like(tail_rows)
    )
    term_rows = jnp.where(
        (tail_pos == lengths[:, None])[..., None], new_vector[:, None, :], term_rows
    )
    placed = (
        jnp.zeros((row_count, token_span, lat_width), jnp.float32)
        .at[new_slot]
        .set(term_rows.astype(jnp.float32))
    )
    attended = (weighted / denominator[..., None]).astype(jnp.bfloat16)
    result = jnp.einsum("rhl,hlv->rhv", attended, w_uv, preferred_element_type=jnp.float32)
    new_blocks = lax.psum_scatter(
        placed.astype(jnp.bfloat16), "pool", scatter_dimension=0, tiled=True
    )
    return (result.astype(jnp.bfloat16), new_blocks)


def solution(mesh):
    placed = (
        P(("grp", "pool"), None, None),
        P(("grp", "pool"), None),
        P(("grp", "pool")),
        P(("grp", "pool")),
        P(("grp", "pool"), ("head", "sub"), None),
        P(("grp", "pool"), ("head", "sub"), None),
        P(("grp", "pool"), None),
        P(),
        P(("head", "sub"), None, None),
        P(("head", "sub"), None, None),
    )
    return jax.shard_map(
        per_device,
        mesh=mesh,
        in_specs=placed,
        out_specs=(
            P(("grp", "pool"), ("head", "sub"), None),
            P(("grp", "pool"), ("head", "sub"), None),
        ),
        check_vma=False,
    )
```

profile of v0, /device:TPU:0, one launch (start us, length us, event | category | flops | bytes accessed | tf_op | source)
XLA Modules:
  0.0 185.2 jit_solution(3294416551906482583)
XLA Ops:
  7.2 0.0 copy-start
  7.2 0.8 broadcast_multiply_fusion
  8.0 0.8 copy.41
  8.8 0.1 fusion.38
  8.9 0.1 reshape.291
  9.0 0.7 broadcast_in_dim.54
  9.7 1.0 gather_fusion.2
  10.6 0.1 reshape.294
  10.7 0.1 and_select_fusion
  10.8 11.7 %all_to_all.10 = s32[4,2,8]{2,1,0:T(2,128)S(1)} all-to-all(s32[4,2,8]{2,1,0:T(2,128)S(1)} %and_select_fusion), channel_id=1, replica_groups=mesh['grp'=2,'pool'=4,'head'=2,'sub'=2] {'pool'}, dimensions={0} | all-to-all | bytes 512 | tf_op jit(solution)/shard_map/all_to_all | solution.py:66
  22.5 0.1 reshape.279
  22.6 0.0 copy-done
  22.6 3.5 %gather_fusion = bf16[64,64,576]{2,1,0:T(8,128)(2,1)} fusion(bf16[24,64,576]{2,1,0:T(8,128)(2,1)S(1)} %copy-done, s32[1024]{0:T(1024)S(1)} %pad_clamp_fusion), kind=kCustom, calls=%fused_computation | custom fusion | bytes 9437440 | tf_op jit(solution)/shard_map/gather | solution.py:67
  26.1 0.0 copy-start.4
  26.1 0.0 copy-start.1
  26.2 5.2 %all-to-all-start.1 = ((bf16[4,2,8,64,576]{4,3,2,1,0:T(8,128)(2,1)}), bf16[4,2,8,64,576]{4,3,2,1,0:T(8,128)(2,1)}, u32[]{:S(2)}, u32[]{:S(2)}) async-start(bf16[4,2,8,64,576]{4,3,2,1,0:T(8,128)(2,1)} %bitcast.68), calls=%async_computation.1 | async-start | bytes 10485760 | tf_op jit(solution)/shard_map/all_to_all | solution.py:68
  31.4 0.0 reduce-scatter.2.cloned.1.call-start
  31.5 0.0 copy-done.3
  31.5 0.1 multiply_subtract_fusion.1
  31.6 0.1 fusion.58
  31.7 0.1 fusion.32
  31.8 0.1 fusion.59
  32.0 0.1 and_select_fusion.5
  32.0 0.1 multiply_subtract_fusion
  32.1 0.2 fusion.31
  32.3 0.1 add_compare_fusion.2
  32.4 0.1 add_multiply_fusion
  32.5 0.1 add_compare_fusion
  32.6 2.8 %fusion.13 = bf16[2,32,512]{2,0,1:T(2,128)(2,1)S(1)} fusion(bf16[32,128,512]{2,1,0:T(8,128)(2,1)} %param.18, bf16[2,32,128]{2,1,0:T(8,128)(2,1)S(1)} %copy-done.1), kind=kOutput, calls=%fused_computation.12 | convolution fusion | flops 8421376 | bytes 4276224 | tf_op jit(solution)/shard_map/rhn,hnl->rhl/dot_general | solution.py:47
  35.5 0.1 fusion.26
  35.6 110.3 %all-to-all-done.1 = bf16[4,2,8,64,576]{4,3,2,1,0:T(8,128)(2,1)} async-done(((bf16[4,2,8,64,576]{4,3,2,1,0:T(8,128)(2,1)}), bf16[4,2,8,64,576]{4,3,2,1,0:T(8,128)(2,1)}, u32[]{:S(2)}, u32[]{:S(2)}) %all-to-all-start.1) | async-done | bytes 4718624 | tf_op jit(solution)/shard_map/all_to_all | solution.py:68
  145.9 4.2 %fusion.15 = f32[2,32,4,8,64]{4,1,3,2,0:T(8,128)S(1)} fusion(f32[2,32,32]{2,1,0:T(8,128)S(1)} %get-tuple-element.21, f32[2,32,32]{2,1,0:T(8,128)S(1)} %get-tuple-element.20, bf16[4,2,8,64,576]{4,3,2,1,0:T(8,128)(2,1)} %all-to-all-done.1), kind=kOutput, calls=%fused_computation.15 | convolution fusion | flops 100667392 | bytes 1589248 | tf_op jit(solution)/shard_map/oktie,khe->khoti/dot_general | solution.py:77
  150.1 4.3 %select_reduce_fusion.1 = (f32[2,32,4]{1,2,0:T(4,128)S(1)}, f32[2,32,4,8,64]{4,1,3,2,0:T(8,128)S(1)}) fusion(pred[2,4,8,64]{3,2,1,0:T(8,128)(4,1)S(1)} %add_compare_fusion, f32[2,32,4,8,64]{4,1,3,2,0:T(8,128)S(1)} %fusion.15, bf16[2,32,512]{2,0,1:T(2,128)(2,1)S(1)} %fusion.13, bf16[4,2,8,64,576]{4,3,2,1,0:T(8,128)(2,1)} %all-to-all-done.1), kind=kOutput, calls=%fused_computation.20 | convolution fusion | flops 134741760 | bytes 5313536 | tf_op jit(solution)/shard_map/oktil,khl->khoti/dot_general | solution.py:71
  154.4 0.5 convert_reduce_fusion
  155.0 0.1 copy.28
  155.1 0.1 copy.29
  155.2 0.1 copy.39
  155.3 3.1 %gather_fusion.1 = bf16[2,64,576]{2,1,0:T(8,128)(2,1)S(1)} fusion(bf16[4,2,8,64,576]{4,3,2,1,0:T(8,128)(2,1)} %all-to-all-done.1, s32[2]{0:T(128)S(1)} %get-tuple-element.14), kind=kCustom, calls=%fused_computation.1 | custom fusion | bytes 294936 | tf_op jit(solution)/shard_map/gather | solution.py:108
  158.3 0.1 select_convert_fusion.2
  158.5 0.6 scatter_fusion
  159.1 0.7 convert_element_type.78
  159.8 0.0 reduce-scatter.2.cloned.1.call-update
  159.8 0.0 copy-start.6
  159.8 3.2 %fusion.10 = f32[2,32,4,512]{3,1,2,0:T(8,128)S(1)} fusion(f32[2,32,4,8,64]{4,1,3,2,0:T(8,128)S(1)} %get-tuple-element.32, f32[2,32,4]{1,2,0:T(4,128)S(1)} %get-tuple-element.31, pred[2,4,8,64]{3,2,1,0:T(8,128)(4,1)S(1)} %add_compare_fusion, bf16[4,2,8,64,576]{4,3,2,1,0:T(8,128)(2,1)} %all-to-all-done.1), kind=kOutput, calls=%fused_computation.10 | convolution fusion | flops 134610944 | bytes 5248000 | tf_op jit(solution)/shard_map/khoti,oktil->khol/dot_general | solution.py:92
  163.0 1.3 fusion.17
  164.4 0.7 fusion.14
  165.1 0.6 copy.30
  165.8 12.6 %reduce-scatter.2.cloned.1.call-done = bf16[2,16,576]{2,1,0:T(8,128)(2,1)} async-done(((bf16[8,16,576]{2,1,0:T(8,128)(2,1)}), bf16[2,16,576]{2,1,0:T(8,128)(2,1)}) %reduce-scatter.2.cloned.1.call-update) | async-done | bytes 36880 | tf_op jit(solution)/shard_map/reduce_scatter | solution.py:124
  (27 shorter events, 0.2 us)
Async XLA Ops:
  7.2 15.5 %copy-start = (bf16[24,64,576]{2,1,0:T(8,128)(2,1)S(1)}, bf16[24,64,576]{2,1,0:T(8,128)(2,1)}, u32[]{:S(2)}) copy-start(bf16[24,64,576]{2,1,0:T(8,128)(2,1)} %param.10) | copy-start | bytes 5308420
  26.1 5.3 %copy-start.2 = (bf16[2,32,64]{2,1,0:T(8,128)(2,1)S(1)}, bf16[2,32,64]{2,1,0:T(8,128)(2,1)}, u32[]{:S(2)}) copy-start(bf16[2,32,64]{2,1,0:T(8,128)(2,1)} %param.15) | copy-start | bytes 24580
  26.1 5.3 %copy-start.5 = (bf16[512]{0:T(512)(128)(2,1)S(1)}, bf16[512]{0:T(512)(128)(2,1)}, u32[]{:S(2)}) copy-start(bf16[512]{0:T(512)(128)(2,1)} %param.17) | copy-start | bytes 3076
  26.1 5.4 %copy-start.3 = (bf16[2,576]{1,0:T(2,128)(2,1)S(1)}, bf16[2,576]{1,0:T(2,128)(2,1)}, u32[]{:S(2)}) copy-start(bf16[2,576]{1,0:T(2,128)(2,1)} %param.16) | copy-start | bytes 6916
  26.1 5.8 %copy-start.7 = (s32[2]{0:T(128)S(1)}, s32[2]{0:T(128)}, u32[]{:S(2)}) copy-start(s32[2]{0:T(128)} %param.13) | copy-start | bytes 28
  26.1 6.2 %copy-start.4 = (s32[2]{0:T(128)S(1)}, s32[2]{0:T(128)}, u32[]{:S(2)}) copy-start(s32[2]{0:T(128)} %param.12) | copy-start | bytes 28
  26.1 6.5 %copy-start.1 = (bf16[2,32,128]{2,1,0:T(8,128)(2,1)S(1)}, bf16[2,32,128]{2,1,0:T(8,128)(2,1)}, u32[]{:S(2)}) copy-start(bf16[2,32,128]{2,1,0:T(8,128)(2,1)} %param.14) | copy-start | bytes 49156
  26.2 119.7 %all-to-all-start.1 = ((bf16[4,2,8,64,576]{4,3,2,1,0:T(8,128)(2,1)}), bf16[4,2,8,64,576]{4,3,2,1,0:T(8,128)(2,1)}, u32[]{:S(2)}, u32[]{:S(2)}) async-start(bf16[4,2,8,64,576]{4,3,2,1,0:T(8,128)(2,1)} %bitcast.68), calls=%async_computation.1 | async-start | bytes 10485760 | tf_op jit(solution)/shard_map/all_to_all | solution.py:68
  31.4 147.0 %reduce-scatter.2.cloned.1.call-start = ((), (), s32[]{:S(2)}) async-start(), calls=%async_computation.3 | async-start | bytes 204800 | tf_op jit(solution)/shard_map/reduce_scatter | solution.py:124
  159.8 4.6 %copy-start.6 = (bf16[32,512,128]{2,1,0:T(8,128)(2,1)S(1)}, bf16[32,512,128]{2,1,0:T(8,128)(2,1)}, u32[]{:S(2)}) copy-start(bf16[32,512,128]{2,1,0:T(8,128)(2,1)} %param.19) | copy-start | bytes 12582916
Sparse Core Ops, SparseCore 0:
  159.9 18.4 reduce-scatter.1
where the time goes:
time: 186 us; the launch traced here: 185 us
  waiting for transfers between devices  123 us (66%)
  matrix products  17 us (9%)
  between operations  14.3 us (8%)
  blocking collectives  11.7 us (6%)
  local copies, waits for them, and re-layouts  10.8 us (6%)
  starting transfers between devices  5.23 us (3%)
  other arithmetic  3.24 us (2%)
    all_to_all x1, waiting for transfers between devices, per_device(): lax.all_to_all(outgoing, 'pool', split_axis=0, concat_axis=0, tiled=True)  110 us
    reduce_scatter x1, waiting for transfers between devices, per_device(): lax.psum_scatter(placed.astype(jnp.bfloat16), 'pool', scatter_dimension=0...  12.6 us
    all_to_all x1, blocking collectives, per_device(): lax.all_to_all(wanted % slot_count, 'pool', split_axis=0, concat_axis=0,...  11.7 us
    all_to_all x1, starting transfers between devices, per_device(): lax.all_to_all(outgoing, 'pool', split_axis=0, concat_axis=0, tiled=True)  5.19 us
    dot_general x1, matrix products, per_device(): jnp.einsum('oktil,khl->khoti', fetched[..., :latent_width], query_lat, pr...  4.33 us
    dot_general x1, matrix products, per_device(): jnp.einsum('oktie,khe->khoti', fetched[..., latent_width:], query_rot, pr...  4.19 us
  transfers between devices with their start and end apart: 2, of which 2 were waited for; matrix products, arithmetic and copies ran while one was open for 5% of the time, Pallas kernels for 0%

commit v1 on v0

v1 whole, which is shorter than its diff:
```python
import functools

import jax
import jax.numpy as jnp
import numpy as np
from jax import lax
from jax.experimental import pallas as pl
from jax.experimental.pallas import tpu as pltpu
from jax.sharding import PartitionSpec as P

EPS = 1e-06
SCALE = 192.0 ** (-0.5)
NONE = -1e30
BF = jnp.bfloat16
F32 = jnp.float32
LANES = 128
META = 32
NEW, TAIL_LEN, DEST, DEST_SLOT, COUNT = 0, 10, 12, 14, 16


def lane_ids(shape):
    return lax.broadcasted_iota(jnp.int32, shape, len(shape) - 1)


def row_ids(shape):
    return lax.broadcasted_iota(jnp.int32, shape, len(shape) - 2)


def rounded(values):
    return values.astype(BF).astype(F32)


def doubled(values):
    return jnp.concatenate([values, values], axis=-1)


def load_kernel(sources, targets, sems):
    copies = [
        pltpu.make_async_copy(source, target, sems.at[n])
        for n, (source, target) in enumerate(zip(sources, targets))
    ]
    for copy in copies:
        copy.start()
    for copy in copies:
        copy.wait()


def query_kernel(wide, *refs):
    sources = refs[:8]
    message, home = refs[8:10]
    targets = refs[10:18]
    meta, sems = refs[18:]
    load_kernel(sources, targets, sems)
    table, lengths, new_slot, q_nope, q_rope, new_latent, gain, freq = targets
    rows, heads, nope = q_nope.shape
    maxblk = table.shape[1]
    kvl = new_latent.shape[1] - q_rope.shape[2]
    queries = rows * heads
    whole = [q_nope[i].astype(F32) for i in range(rows)]

    lane = lane_ids((rows, LANES))
    row = row_ids((rows, LANES))
    position = jnp.full((rows, LANES), lengths[0], jnp.int32)
    for i in range(1, rows):
        position = jnp.where(row == i, lengths[i], position)
    angle = position.astype(F32) * freq[...]
    cosine = jnp.cos(angle)
    sine = jnp.sin(angle)
    sine = jnp.where(lane % 64 < 32, -sine, sine)
    qlane = lane_ids((heads, LANES))
    for i in range(rows):
        raw = doubled(q_rope[i].astype(F32))
        turned = raw * cosine[i : i + 1] + pltpu.roll(raw, 32, 1) * sine[i : i + 1]
        high = rounded(turned)
        whole.append(jnp.where(qlane < 64, high, turned - high))
    message[0 : 2 * queries, :] = jnp.concatenate(whole, axis=0).astype(BF)

    latent = new_latent[:, :kvl].astype(F32)
    square = jnp.mean(latent * latent, axis=-1, keepdims=True)
    gains = gain[...].astype(F32)
    gains = jnp.concatenate([gains[c : c + 1] for c in range(kvl // LANES)], axis=1)
    new_c = rounded(latent * lax.rsqrt(square + EPS) * gains)
    key = doubled(new_latent[:, kvl:].astype(F32))
    key = key * cosine + pltpu.roll(key, 32, 1) * sine
    home[...] = jnp.zeros_like(home)
    home[0:rows, 0:kvl] = new_c
    home[0:rows, kvl : kvl + LANES] = key
    meta[...] = jnp.zeros_like(meta)
    for c in range(kvl // LANES):
        meta[NEW + rows * c : NEW + rows * (c + 1), :] = new_c[:, c * LANES : (c + 1) * LANES]
    c = kvl // LANES
    meta[NEW + rows * c : NEW + rows * (c + 1), :] = key

    one = lane_ids((1, LANES))
    for i in range(rows):
        length = lengths[i]
        slot = new_slot[i]
        tail = table[i, length // 64]
        meta[TAIL_LEN + i : TAIL_LEN + i + 1, :] = jnp.full((1, LANES), length % 64, jnp.int32).astype(F32)
        meta[DEST + i : DEST + i + 1, :] = jnp.full((1, LANES), slot // rows, jnp.int32).astype(F32)
        meta[DEST_SLOT + i : DEST_SLOT + i + 1, :] = jnp.full((1, LANES), slot % rows, jnp.int32).astype(F32)
        counts = [jnp.zeros((1, LANES), jnp.int32) for _ in range(wide)]
        for j in range(maxblk):
            block = table[i, j]
            count = jnp.clip(length - 64 * j, 0, 64)
            for w in range(wide):
                counts[w] = counts[w] + jnp.where(one + w * LANES == block, count, 0)
        for w in range(wide):
            meta[COUNT + rows * w + i : COUNT + rows * w + i + 1, :] = counts[w].astype(F32)
            at = COUNT + rows * (wide + w) + i
            meta[at : at + 1, :] = jnp.where(one + w * LANES == tail, 1.0, 0.0)
    message[2 * queries : 2 * queries + META, :] = meta[...].astype(BF)


def attend_kernel(owners, head_parts, rows, heads, *refs):
    messages = refs[:owners]
    home, pool, w_uk, w_uv = refs[owners : owners + 4]
    replies = refs[owners + 4 : 2 * owners + 4]
    q_flat, lat, scores, out, meta = refs[2 * owners + 4 :]
    slots, block, width = pool.shape
    tokens = slots * block
    kvl = w_uk.shape[2]
    tiles = kvl // LANES
    queries = rows * heads
    everyone = owners * rows
    wide = (owners * slots + LANES - 1) // LANES
    me = lax.axis_index("pool")
    part = lax.axis_index(("head", "sub"))

    for k in range(owners):
        q_flat[k * queries : (k + 1) * queries, :] = messages[k][0:queries, :].astype(F32)
        meta[k] = messages[k][2 * queries : 2 * queries + META, :].astype(F32)

    for h in range(heads):
        one_head = q_flat[pl.ds(h, everyone, stride=heads), :].astype(BF)
        absorbed = jnp.dot(one_head, w_uk[h], preferred_element_type=F32)
        for c in range(tiles):
            lat[c, pl.ds(h, everyone, stride=heads), :] = absorbed[:, c * LANES : (c + 1) * LANES]

    lane = lane_ids((LANES, tokens))
    counts = jnp.zeros((everyone, tokens), F32)
    for w in range(wide):
        count_rows = jnp.concatenate(
            [meta[k, COUNT + rows * w : COUNT + rows * (w + 1), :] for k in range(owners)], axis=0
        ).astype(BF)
        here = jnp.where(
            row_ids((LANES, tokens)) + w * LANES == me * slots + lane // block, 1.0, 0.0
        ).astype(BF)
        counts = counts + jnp.dot(count_rows, here, preferred_element_type=F32)
    within = (lane_ids((everyone, tokens)) % block).astype(F32)
    bias = jnp.where(within < counts, 0.0, NONE)

    rotated = [messages[k][queries : 2 * queries, :] for k in range(owners)]
    turned = jnp.concatenate(rotated, axis=0) if owners > 1 else rotated[0]
    key_dims = (((1,), (1,)), ((), ()))
    flat_pool = pool[...].reshape(tokens, width)
    full = jnp.concatenate(
        [lat[c].astype(BF) for c in range(tiles)] + [turned[:, 0 : width - kvl]], axis=1
    )
    scores[...] = lax.dot_general(full, flat_pool, key_dims, preferred_element_type=F32)
    scores[...] += lax.dot_general(
        turned[:, width - kvl :], flat_pool[:, kvl:], key_dims, preferred_element_type=F32
    )

    own = rotated[0].astype(F32)
    biggest, totals, weights, new_weights = [], [], [], []
    for r in range(everyone):
        some = scores[r * heads : (r + 1) * heads, :] * SCALE + bias[r : r + 1, :]
        top = jnp.max(some, axis=1, keepdims=True)
        if r < rows:
            new_score = jnp.zeros((heads, LANES), F32)
            for c in range(tiles):
                mine = rounded(lat[c, r * heads : (r + 1) * heads, :])
                new_score = new_score + mine * home[r : r + 1, c * LANES : (c + 1) * LANES]
            new_score = jnp.sum(new_score, axis=1, keepdims=True)
            both = own[r * heads : (r + 1) * heads, :]
            both = both + pltpu.roll(both, 64, 1)
            new_score = SCALE * (
                new_score
                + 0.5 * jnp.sum(both * home[r : r + 1, kvl : kvl + LANES], axis=1, keepdims=True)
            )
            top = jnp.maximum(top, new_score)
        weight = jnp.exp(some - top).astype(BF)
        total = jnp.sum(weight.astype(F32), axis=1, keepdims=True)
        if r < rows:
            new_weight = rounded(jnp.exp(new_score - top))
            total = total + new_weight
            new_weights.append(new_weight)
        else:
            total = jnp.where(top > 0.5 * NONE, total, 0.0)
        biggest.append(top)
        totals.append(total)
        weights.append(weight)
    values = flat_pool[:, :kvl]
    sums = jnp.dot(jnp.concatenate(weights, axis=0), values, preferred_element_type=F32)
    for r in range(everyone):
        some = sums[r * heads : (r + 1) * heads, :]
        if r < rows:
            some = some + new_weights[r] * home[r : r + 1, 0:kvl]
        share = jnp.where(totals[r] > 0.0, 1.0 / jnp.maximum(totals[r], 1e-30), 0.0)
        some = some * share
        for c in range(tiles):
            lat[c, r * heads : (r + 1) * heads, :] = some[:, c * LANES : (c + 1) * LANES]

    for h in range(heads):
        one_head = jnp.concatenate(
            [lat[c, pl.ds(h, everyone, stride=heads), :] for c in range(tiles)], axis=1
        ).astype(BF)
        out[pl.ds(h, everyone, stride=heads), :] = jnp.dot(
            one_head, w_uv[h], preferred_element_type=F32
        )

    span = block // head_parts
    tails = everyone * span
    if span % 16 == 0:
        near_span, first = span, part * span
        near_pool = pool[:, pl.ds(pl.multiple_of(first, span), span), :]
        near_pool = near_pool.reshape(slots * span, width)
    else:
        near_span, first = block, 0
        near_pool = flat_pool
    near = slots * near_span
    where_from = first + lane_ids((1, near)) % near_span
    place = row_ids((tails, near))
    diagonal = part * span + place % span == first + lane_ids((tails, near)) % near_span
    chosen = jnp.zeros((tails, near), F32)
    new_rows = [jnp.zeros((tails, LANES), F32) for _ in range(kvl // LANES + 1)]
    token = part * span + row_ids((tails, LANES)) % span
    for k in range(owners):
        dest = meta[k, DEST : DEST + rows, :]
        dest = me.astype(F32) - dest
        dest = jnp.where(dest < 0.0, dest + owners, dest)
        dest = dest * rows + meta[k, DEST_SLOT : DEST_SLOT + rows, :]
        tail_len = meta[k, TAIL_LEN : TAIL_LEN + rows, :]
        is_last = jnp.zeros((rows, near), F32)
        for w in range(wide):
            here = jnp.where(
                row_ids((LANES, near)) + w * LANES == me * slots + lane_ids((LANES, near)) // near_span,
                1.0,
                0.0,
            ).astype(BF)
            at = COUNT + rows * (wide + w)
            is_last = is_last + jnp.dot(
                meta[k, at : at + rows, :].astype(BF), here, preferred_element_type=F32
            )
        is_holder = jnp.max(is_last, axis=1, keepdims=True)
        for i in range(rows):
            old = jnp.where(
                where_from.astype(F32) < tail_len[i : i + 1, 0:1],
                is_last[i : i + 1, :],
                0.0,
            )
            goes = (place // span).astype(F32) == dest[i : i + 1, 0:1]
            chosen = chosen + jnp.where(goes, old, 0.0)
            new_here = (
                ((row_ids((tails, LANES)) // span).astype(F32) == dest[i : i + 1, :])
                & (token.astype(F32) == tail_len[i : i + 1, :])
                & (is_holder[i : i + 1, :] > 0.5)
            )
            for c in range(kvl // LANES + 1):
                new_rows[c] = new_rows[c] + jnp.where(
                    new_here, meta[k, NEW + rows * c + i : NEW + rows * c + i + 1, :], 0.0
                )
    chosen = jnp.where(diagonal, chosen, 0.0).astype(BF)
    tail_rows = jnp.dot(chosen, near_pool, preferred_element_type=F32)

    send_lane = lane_ids((heads, LANES))
    tail_lane = lane_ids((rows * span, LANES))
    for k in range(owners):
        mine = slice(k * rows * span, (k + 1) * rows * span)
        whole = [out[k * queries : (k + 1) * queries, :]]
        for c in range(tiles):
            whole.append(tail_rows[mine, c * LANES : (c + 1) * LANES] + new_rows[c][mine, :])
        last = doubled(tail_rows[mine, kvl:]) + new_rows[tiles][mine, :]
        stats = jnp.zeros((heads, LANES), F32)
        for i in range(rows):
            for n, value in enumerate((biggest[k * rows + i], totals[k * rows + i])):
                for piece in range(3):
                    high = rounded(value)
                    stats = jnp.where(send_lane == 64 + 6 * i + 3 * n + piece, high, stats)
                    value = value - high
        whole.append(jnp.where(tail_lane < 64, last, stats))
        whole = jnp.concatenate(whole, axis=0)
        missing = replies[k].shape[0] - whole.shape[0]
        if missing:
            whole = jnp.concatenate([whole, jnp.zeros((missing, LANES), F32)], axis=0)
        replies[k][...] = whole.astype(BF)


def combine_kernel(rows, heads, span, *refs):
    replies = [reply[...].astype(F32) for reply in refs[:-2]]
    attn_out, new_blocks = refs[-2:]
    kvl_tiles = new_blocks.shape[2] // LANES
    queries = rows * heads
    last = queries + kvl_tiles * rows * span
    stats = [reply[last : last + heads, :] for reply in replies]
    for i in range(rows):
        tops, totals = [], []
        for stat in stats:
            at = 64 + 6 * i
            tops.append(stat[:, at : at + 1] + stat[:, at + 1 : at + 2] + stat[:, at + 2 : at + 3])
            at = at + 3
            totals.append(stat[:, at : at + 1] + stat[:, at + 1 : at + 2] + stat[:, at + 2 : at + 3])
        top = functools.reduce(jnp.maximum, tops)
        shares = [jnp.exp(t - top) * total for t, total in zip(tops, totals)]
        denominator = functools.reduce(jnp.add, shares)
        result = jnp.zeros((heads, LANES), F32)
        for share, reply in zip(shares, replies):
            result = result + share * reply[i * heads : (i + 1) * heads, :]
        attn_out[i] = (result / denominator).astype(BF)
    for c in range(kvl_tiles + 1):
        at = queries + c * rows * span
        tile = replies[0][at : at + rows * span, :]
        for reply in replies[1:]:
            tile = tile + reply[at : at + rows * span, :]
        left = min(LANES, new_blocks.shape[2] - c * LANES)
        for i in range(rows):
            new_blocks[i, :, c * LANES : c * LANES + left] = tile[
                i * span : (i + 1) * span, 0:left
            ].astype(BF)


def per_device(
    pool, block_table, lengths, new_slot, q_nope, q_rope, new_latent, kv_gain, w_uk, w_uv
):
    owners = lax.axis_size("pool")
    parts = lax.axis_size(("head", "sub"))
    slots, block, width = pool.shape
    rows, heads, nope = q_nope.shape
    rope = q_rope.shape[2]
    kvl = kv_gain.shape[0]
    vdim = w_uv.shape[2]
    queries = rows * heads
    everyone = owners * rows
    wide = (owners * slots + LANES - 1) // LANES
    span = block // parts
    tokens = slots * block
    vmem = pl.BlockSpec(memory_space=pltpu.VMEM)
    hbm = pl.BlockSpec(memory_space=pltpu.HBM)

    half = rope // 2
    freq = 10000.0 ** (-(np.arange(LANES) % half).astype(np.float32) / np.float32(half))
    freq = jnp.asarray(freq.astype(np.float32)[None])
    gain = kv_gain.reshape(-1, LANES)
    raw = (block_table, lengths, new_slot, q_nope, q_rope, new_latent, gain, freq)
    raw = [pltpu.with_memory_space_constraint(a, pltpu.HBM) for a in raw]
    message, home = pl.pallas_call(
        functools.partial(query_kernel, wide),
        out_shape=(
            pltpu.VMEM((2 * queries + META, LANES), BF),
            pltpu.VMEM((8, kvl + LANES), F32),
        ),
        in_specs=[hbm] * len(raw),
        out_specs=(vmem, vmem),
        scratch_shapes=[
            (pltpu.SMEM if n < 3 else pltpu.VMEM)(a.shape, a.dtype) for n, a in enumerate(raw)
        ]
        + [pltpu.VMEM((META, LANES), F32), pltpu.SemaphoreType.DMA((len(raw),))],
        compiler_params=pltpu.CompilerParams(vmem_limit_bytes=4 * 2**20),
        name="queries",
    )(*raw)

    def ring(step):
        return [(i, (i + step) % owners) for i in range(owners)]

    messages = [message]
    for k in range(1, owners):
        messages.append(lax.ppermute(message, "pool", ring(k)))

    near = pl.pallas_call(
        lambda *refs: load_kernel(refs[:3], refs[3:6], refs[6]),
        out_shape=tuple(pltpu.VMEM(a.shape, a.dtype) for a in (w_uk, pool, w_uv)),
        in_specs=[hbm] * 3,
        out_specs=(vmem,) * 3,
        scratch_shapes=[pltpu.SemaphoreType.DMA((3,))],
        compiler_params=pltpu.CompilerParams(vmem_limit_bytes=2**20),
        cost_estimate=pl.CostEstimate(flops=0, bytes_accessed=20 * 2**20, transcendentals=0),
        name="load",
    )(*[pltpu.with_memory_space_constraint(a, pltpu.HBM) for a in (w_uk, pool, w_uv)])

    reply_rows = -(-(queries + (kvl // LANES + 1) * rows * span) // 16) * 16
    replies = pl.pallas_call(
        functools.partial(attend_kernel, owners, parts, rows, heads),
        out_shape=tuple(
            jax.ShapeDtypeStruct((reply_rows, LANES), BF) for _ in range(owners)
        ),
        in_specs=[vmem] * (owners + 4),
        out_specs=tuple([vmem] * owners),
        scratch_shapes=[
            pltpu.VMEM((owners * queries, nope), F32),
            pltpu.VMEM((kvl // LANES, owners * queries, LANES), F32),
            pltpu.VMEM((owners * queries, tokens), F32),
            pltpu.VMEM((owners * queries, vdim), F32),
            pltpu.VMEM((owners, META, LANES), F32),
        ],
        compiler_params=pltpu.CompilerParams(vmem_limit_bytes=24 * 2**20),
        name="attend",
    )(*messages, home, near[1], near[0], near[2])

    returned = [replies[0]]
    for k in range(1, owners):
        returned.append(lax.ppermute(replies[k], "pool", ring(-k)))

    return pl.pallas_call(
        functools.partial(combine_kernel, rows, heads, span),
        out_shape=(
            jax.ShapeDtypeStruct((rows, heads, vdim), BF),
            jax.ShapeDtypeStruct((rows, span, width), BF),
        ),
        in_specs=[vmem] * owners,
        out_specs=(vmem, vmem),
        compiler_params=pltpu.CompilerParams(vmem_limit_bytes=4 * 2**20),
        name="combine",
    )(*returned)


def solution(mesh):
    placed = (
        P(("grp", "pool"), None, None),
        P(("grp", "pool"), None),
        P(("grp", "pool")),
        P(("grp", "pool")),
        P(("grp", "pool"), ("head", "sub"), None),
        P(("grp", "pool"), ("head", "sub"), None),
        P(("grp", "pool"), None),
        P(),
        P(("head", "sub"), None, None),
        P(("head", "sub"), None, None),
    )
    return jax.shard_map(
        per_device,
        mesh=mesh,
        in_specs=placed,
        out_specs=(
            P(("grp", "pool"), ("head", "sub"), None),
            P(("grp", "pool"), ("head", "sub"), None),
        ),
        check_vma=False,
    )
```

time: 186 us -> 27 us (0.15)
  waiting for transfers between devices: 123 us -> 6.68 us
  matrix products: 17 us -> 0 us
  between operations: 14.3 us -> 0.68 us
  blocking collectives: 11.7 us -> 0 us
  local copies, waits for them, and re-layouts: 10.8 us -> 0 us
  Pallas kernels: 0 us -> 10.1 us
  starting transfers between devices: 5.23 us -> 9.42 us
  other arithmetic: 3.24 us -> 0 us
    all_to_all x1 -> x0, waiting for transfers between devices: 110 us -> none  [per_device(): lax.all_to_all(outgoing, 'pool', split_axis=0, concat_axis=0, tiled=True)]
    dot_general x8 -> x0, matrix products: 17 us -> none  [the longest x1 4.33 us: per_device(): jnp.einsum('oktil,khl->khoti', fetched[..., :latent_width], query_lat, pr...]
    reduce_scatter x1 -> x0, waiting for transfers between devices: 12.6 us -> none  [per_device(): lax.psum_scatter(placed.astype(jnp.bfloat16), 'pool', scatter_dimension=0...]
    all_to_all x1 -> x0, blocking collectives: 11.7 us -> none  [per_device(): lax.all_to_all(wanted % slot_count, 'pool', split_axis=0, concat_axis=0,...]
    pallas_call x0 -> x4, Pallas kernels: none -> 10.1 us  [the longest x1 4.14 us: per_device(): pl.pallas_call(functools.partial(attend_kernel, owners, parts, rows, head...]
    ppermute x0 -> x6, starting transfers between devices: none -> 9.42 us  [the longest x3 6.11 us: per_device(): messages.append(lax.ppermute(message, 'pool', ring(k)))]
    gather x5 -> x0, local copies, waits for them, and re-layouts: 7.7 us -> none  [the longest x1 3.5 us: per_device(): outgoing = pool[requested]]
    ppermute x0 -> x6, waiting for transfers between devices: none -> 6.68 us  [the longest x3 5.97 us: per_device(): returned.append(lax.ppermute(replies[k], 'pool', ring(-k)))]
  transfers between devices with their start and end apart: 2 -> 6, of which waited for: 2 -> 4; matrix products, arithmetic and copies ran while one was open for 5% -> 0% of each run, Pallas kernels for 0% -> 15%
where the time goes in v1:
time: 27 us; the launch traced here: 26.9 us
  Pallas kernels  10.1 us (37%)
  starting transfers between devices  9.42 us (35%)
  waiting for transfers between devices  6.68 us (25%)
  between operations  0.68 us (3%)
    ppermute x3, starting transfers between devices, per_device(): messages.append(lax.ppermute(message, 'pool', ring(k)))  6.11 us
    ppermute x3, waiting for transfers between devices, per_device(): returned.append(lax.ppermute(replies[k], 'pool', ring(-k)))  5.97 us
    pallas_call x1, Pallas kernels, per_device(): pl.pallas_call(functools.partial(attend_kernel, owners, parts, rows, head...  4.14 us
    pallas_call x1, Pallas kernels, per_device(): pl.pallas_call(lambda *refs: load_kernel(refs[:3], refs[3:6], refs[6]), o...  4.06 us
    ppermute x3, starting transfers between devices, per_device(): returned.append(lax.ppermute(replies[k], 'pool', ring(-k)))  3.31 us
    pallas_call x1, Pallas kernels, per_device(): pl.pallas_call(functools.partial(query_kernel, wide), out_shape=(pltpu.VM...  1.01 us
    pallas_call x1, Pallas kernels, per_device(): pl.pallas_call(functools.partial(combine_kernel, rows, heads, span), out_...  0.87 us
    ppermute x3, waiting for transfers between devices, per_device(): messages.append(lax.ppermute(message, 'pool', ring(k)))  0.71 us
  transfers between devices with their start and end apart: 6, of which 4 were waited for; matrix products, arithmetic and copies ran while one was open for 0% of the time, Pallas kernels for 15%

profile of v1, /device:TPU:0, one launch (start us, length us, event | category | flops | bytes accessed | tf_op | source)
XLA Modules:
  0.0 26.9 jit_solution(8167977816075339610)
XLA Ops:
  0.6 1.0 %queries.1 = (bf16[160,128]{1,0:T(8,128)(2,1)S(1)}, f32[8,640]{1,0:T(8,128)S(1)}) custom-call(s32[2,32]{1,0:T(2,128)} %refs_0_.2, s32[2]{0:T(128)} %refs_1_.2, s32[2]{0:T(128)} %refs_2_.2, bf16[2,32,128]{2,1,0:T(8,128)(2,1)} %refs_3_.1, bf16[2,32,64]{2,1,0:T(8,128)(2,1)} %refs_4_.1, bf16[2,576]{1,0:T(2,128)(2,1)} %refs_5_.1, bf16[4,128]{1,0:T(4,128)(2,1)} %bitcast.1, ...), custom_call_target="tpu_custom_call" | custom-call | tf_op jit(solution)/shard_map/queries/pallas_call | solution.py:347
  1.7 5.1 %collective-permute-start.2 = (bf16[160,128]{1,0:T(8,128)(2,1)S(1)}, bf16[160,128]{1,0:T(8,128)(2,1)S(1)}, u32[]{:S(2)}, u32[]{:S(2)}) collective-permute-start(bf16[160,128]{1,0:T(8,128)(2,1)S(1)} %get-tuple-element.11.refs_0_), channel_id=1, source_target_pairs={{0,12},{4,0},{8,4},{12,8},{1,13},{5,1},{9,5},{13,9},{2,14},{6,2},{... | collective-permute-start | bytes 122888 | tf_op jit(solution)/shard_map/ppermute | solution.py:368
  6.8 0.0 collective-permute-start.1
  6.8 1.0 %collective-permute-start = (bf16[160,128]{1,0:T(8,128)(2,1)S(1)}, bf16[160,128]{1,0:T(8,128)(2,1)S(1)}, u32[]{:S(2)}, u32[]{:S(2)}) collective-permute-start(bf16[160,128]{1,0:T(8,128)(2,1)S(1)} %get-tuple-element.11.refs_0_), channel_id=1, source_target_pairs={{0,4},{4,8},{8,12},{12,0},{1,5},{5,9},{9,13},{13,1},{2,6},{6,10},{... | collective-permute-start | bytes 122888 | tf_op jit(solution)/shard_map/ppermute | solution.py:368
  7.8 4.1 %load.1 = (bf16[32,128,512]{2,1,0:T(8,128)(2,1)S(1)}, bf16[24,64,576]{2,1,0:T(8,128)(2,1)S(1)}, bf16[32,512,128]{2,1,0:T(8,128)(2,1)S(1)}) custom-call(bf16[32,128,512]{2,1,0:T(8,128)(2,1)} %refs_0_.3, bf16[24,64,576]{2,1,0:T(8,128)(2,1)} %refs_1_.3, bf16[32,512,128]{2,1,0:T(8,128)(2,1)} %refs_2_.3), custom_call_target="tpu_custom_call" | custom-call | bytes 20971520 | tf_op jit(solution)/shard_map/load/pallas_call | solution.py:370
  11.8 0.0 collective-permute-done.2.refs_3_
  11.8 0.0 collective-permute-done.1.refs_2_
  11.9 0.7 %collective-permute-done.refs_1_ = bf16[160,128]{1,0:T(8,128)(2,1)S(1)} collective-permute-done((bf16[160,128]{1,0:T(8,128)(2,1)S(1)}, bf16[160,128]{1,0:T(8,128)(2,1)S(1)}, u32[]{:S(2)}, u32[]{:S(2)}) %collective-permute-start) | collective-permute-done | bytes 40992 | tf_op jit(solution)/shard_map/ppermute | solution.py:368
  12.6 4.1 %attend.1 = (bf16[224,128]{1,0:T(8,128)(2,1)S(1)}, bf16[224,128]{1,0:T(8,128)(2,1)S(1)}, bf16[224,128]{1,0:T(8,128)(2,1)S(1)}, bf16[224,128]{1,0:T(8,128)(2,1)S(1)}) custom-call(bf16[160,128]{1,0:T(8,128)(2,1)S(1)} %get-tuple-element.11.refs_0_, bf16[160,128]{1,0:T(8,128)(2,1)S(1)} %collective-permute-done.refs_1_, ...), custom_call_target="tpu_custom_call" | custom-call | tf_op jit(solution)/shard_map/attend/pallas_call | solution.py:382
  16.7 2.2 %collective-permute-start.3 = (bf16[224,128]{1,0:T(8,128)(2,1)S(1)}, bf16[224,128]{1,0:T(8,128)(2,1)S(1)}, u32[]{:S(2)}, u32[]{:S(2)}) collective-permute-start(bf16[224,128]{1,0:T(8,128)(2,1)S(1)} %get-tuple-element.17), channel_id=1, source_target_pairs={{0,12},{4,0},{8,4},{12,8},{1,13},{5,1},{9,5},{13,9},{2,14},{6,2},{... | collective-permute-start | bytes 172040 | tf_op jit(solution)/shard_map/ppermute | solution.py:402
  18.9 1.1 %collective-permute-start.4 = (bf16[224,128]{1,0:T(8,128)(2,1)S(1)}, bf16[224,128]{1,0:T(8,128)(2,1)S(1)}, u32[]{:S(2)}, u32[]{:S(2)}) collective-permute-start(bf16[224,128]{1,0:T(8,128)(2,1)S(1)} %get-tuple-element.18), channel_id=1, source_target_pairs={{0,8},{4,12},{8,0},{12,4},{1,9},{5,13},{9,1},{13,5},{2,10},{6,14},... | collective-permute-start | bytes 172040 | tf_op jit(solution)/shard_map/ppermute | solution.py:402
  20.0 0.0 collective-permute-start.5
  20.0 0.9 %collective-permute-done.3.refs_1_ = bf16[224,128]{1,0:T(8,128)(2,1)S(1)} collective-permute-done((bf16[224,128]{1,0:T(8,128)(2,1)S(1)}, bf16[224,128]{1,0:T(8,128)(2,1)S(1)}, u32[]{:S(2)}, u32[]{:S(2)}) %collective-permute-start.3) | collective-permute-done | bytes 57376 | tf_op jit(solution)/shard_map/ppermute | solution.py:402
  20.9 3.6 %collective-permute-done.4.refs_2_ = bf16[224,128]{1,0:T(8,128)(2,1)S(1)} collective-permute-done((bf16[224,128]{1,0:T(8,128)(2,1)S(1)}, bf16[224,128]{1,0:T(8,128)(2,1)S(1)}, u32[]{:S(2)}, u32[]{:S(2)}) %collective-permute-start.4) | collective-permute-done | bytes 57376 | tf_op jit(solution)/shard_map/ppermute | solution.py:402
  24.5 1.5 %collective-permute-done.5.refs_3_ = bf16[224,128]{1,0:T(8,128)(2,1)S(1)} collective-permute-done((bf16[224,128]{1,0:T(8,128)(2,1)S(1)}, bf16[224,128]{1,0:T(8,128)(2,1)S(1)}, u32[]{:S(2)}, u32[]{:S(2)}) %collective-permute-start.5) | collective-permute-done | bytes 57376 | tf_op jit(solution)/shard_map/ppermute | solution.py:402
  26.0 0.9 %combine.1 = (bf16[2,32,128]{2,1,0:T(8,128)(2,1)}, bf16[2,16,576]{2,1,0:T(8,128)(2,1)}) custom-call(bf16[224,128]{1,0:T(8,128)(2,1)S(1)} %get-tuple-element.16.refs_0_, bf16[224,128]{1,0:T(8,128)(2,1)S(1)} %collective-permute-done.3.refs_1_, bf16[224,128]{1,0:T(8,128)(2,1)S(1)} %collective-permute-done.4.refs_2_, ...), custom_call_target="tpu_custom_call" | custom-call | tf_op jit(solution)/shard_map/combine/pallas_call | solution.py:404
Async XLA Ops:
  1.7 10.2 %collective-permute-start.2 = (bf16[160,128]{1,0:T(8,128)(2,1)S(1)}, bf16[160,128]{1,0:T(8,128)(2,1)S(1)}, u32[]{:S(2)}, u32[]{:S(2)}) collective-permute-start(bf16[160,128]{1,0:T(8,128)(2,1)S(1)} %get-tuple-element.11.refs_0_), channel_id=1, source_target_pairs={{0,12},{4,0},{8,4},{12,8},{1,13},{5,1},{9,5},{13,9},{2,14},{6,2},{... | collective-permute-start | bytes 122888 | tf_op jit(solution)/shard_map/ppermute | solution.py:368
  6.8 5.1 %collective-permute-start.1 = (bf16[160,128]{1,0:T(8,128)(2,1)S(1)}, bf16[160,128]{1,0:T(8,128)(2,1)S(1)}, u32[]{:S(2)}, u32[]{:S(2)}) collective-permute-start(bf16[160,128]{1,0:T(8,128)(2,1)S(1)} %get-tuple-element.11.refs_0_), channel_id=1, source_target_pairs={{0,8},{4,12},{8,0},{12,4},{1,9},{5,13},{9,1},{13,5},{2,10},{6,14},... | collective-permute-start | bytes 122888 | tf_op jit(solution)/shard_map/ppermute | solution.py:368
  6.8 5.8 %collective-permute-start = (bf16[160,128]{1,0:T(8,128)(2,1)S(1)}, bf16[160,128]{1,0:T(8,128)(2,1)S(1)}, u32[]{:S(2)}, u32[]{:S(2)}) collective-permute-start(bf16[160,128]{1,0:T(8,128)(2,1)S(1)} %get-tuple-element.11.refs_0_), channel_id=1, source_target_pairs={{0,4},{4,8},{8,12},{12,0},{1,5},{5,9},{9,13},{13,1},{2,6},{6,10},{... | collective-permute-start | bytes 122888 | tf_op jit(solution)/shard_map/ppermute | solution.py:368
  16.7 4.2 %collective-permute-start.3 = (bf16[224,128]{1,0:T(8,128)(2,1)S(1)}, bf16[224,128]{1,0:T(8,128)(2,1)S(1)}, u32[]{:S(2)}, u32[]{:S(2)}) collective-permute-start(bf16[224,128]{1,0:T(8,128)(2,1)S(1)} %get-tuple-element.17), channel_id=1, source_target_pairs={{0,12},{4,0},{8,4},{12,8},{1,13},{5,1},{9,5},{13,9},{2,14},{6,2},{... | collective-permute-start | bytes 172040 | tf_op jit(solution)/shard_map/ppermute | solution.py:402
  18.9 5.6 %collective-permute-start.4 = (bf16[224,128]{1,0:T(8,128)(2,1)S(1)}, bf16[224,128]{1,0:T(8,128)(2,1)S(1)}, u32[]{:S(2)}, u32[]{:S(2)}) collective-permute-start(bf16[224,128]{1,0:T(8,128)(2,1)S(1)} %get-tuple-element.18), channel_id=1, source_target_pairs={{0,8},{4,12},{8,0},{12,4},{1,9},{5,13},{9,1},{13,5},{2,10},{6,14},... | collective-permute-start | bytes 172040 | tf_op jit(solution)/shard_map/ppermute | solution.py:402
  20.0 6.0 %collective-permute-start.5 = (bf16[224,128]{1,0:T(8,128)(2,1)S(1)}, bf16[224,128]{1,0:T(8,128)(2,1)S(1)}, u32[]{:S(2)}, u32[]{:S(2)}) collective-permute-start(bf16[224,128]{1,0:T(8,128)(2,1)S(1)} %get-tuple-element.19), channel_id=1, source_target_pairs={{0,4},{4,8},{8,12},{12,0},{1,5},{5,9},{9,13},{13,1},{2,6},{6,10},{... | collective-permute-start | bytes 172040 | tf_op jit(solution)/shard_map/ppermute | solution.py:402

commit v2 on v1

v2 whole, which is shorter than its diff:
```python
import functools

import jax
import jax.numpy as jnp
import numpy as np
from jax import lax
from jax.experimental import pallas as pl
from jax.experimental.pallas import tpu as pltpu
from jax.sharding import PartitionSpec as P

EPS = 1e-06
SCALE = 192.0 ** (-0.5)
NONE = -1e30
BF = jnp.bfloat16
F32 = jnp.float32
LANES = 128
META = 32
NEW, TAIL_LEN, DEST, DEST_SLOT, COUNT = 0, 5, 6, 7, 8
LOG2E = 1.4426950408889634
ABSORB_UNROLL, SOFTEN_UNROLL, PROJECT_UNROLL = 32, 16, 32


def lane_ids(shape):
    return lax.broadcasted_iota(jnp.int32, shape, len(shape) - 1)


def row_ids(shape):
    return lax.broadcasted_iota(jnp.int32, shape, len(shape) - 2)


def rounded(values):
    return values.astype(BF).astype(F32)


def doubled(values):
    return jnp.concatenate([values, values], axis=-1)


def each_of(count, unroll, body):
    unroll = min(count, unroll)
    if unroll == count:
        for n in range(count):
            body(n)
    else:

        def some(n, carry):
            for m in range(unroll):
                body(n * unroll + m)
            return carry

        lax.fori_loop(0, count // unroll, some, 0)


def copies_of(sources, targets, sems, pieces=1):
    copies = []
    for source, target in zip(sources, targets):
        size = source.shape[0] // pieces
        for n in range(pieces):
            part = pl.ds(n * size, size)
            copies.append(
                pltpu.make_async_copy(source.at[part], target.at[part], sems.at[len(copies)])
            )
    for copy in copies:
        copy.start()
    return copies


def load_kernel(w_uk_hbm, pool_hbm, w_uk, pool, sems):
    for copy in copies_of([w_uk_hbm, pool_hbm], [w_uk, pool], sems, 4):
        copy.wait()


def query_kernel(wide, *refs):
    sources = refs[:8]
    message, home = refs[8:10]
    targets = refs[10:18]
    meta, sems = refs[18:]
    copies = copies_of(sources, targets, sems)
    for copy in copies:
        copy.wait()
    table, lengths, new_slot, q_nope, q_rope, new_latent, gain, freq = targets
    rows, heads, nope = q_nope.shape
    maxblk = table.shape[1]
    kvl = new_latent.shape[1] - q_rope.shape[2]
    queries = rows * heads
    whole = [q_nope[i].astype(F32) for i in range(rows)]

    lane = lane_ids((rows, LANES))
    row = row_ids((rows, LANES))
    position = jnp.full((rows, LANES), lengths[0], jnp.int32)
    for i in range(1, rows):
        position = jnp.where(row == i, lengths[i], position)
    angle = position.astype(F32) * freq[...]
    cosine = jnp.cos(angle)
    sine = jnp.sin(angle)
    sine = jnp.where(lane % 64 < 32, -sine, sine)
    qlane = lane_ids((heads, LANES))
    for i in range(rows):
        raw = doubled(q_rope[i].astype(F32))
        turned = raw * cosine[i : i + 1] + pltpu.roll(raw, 32, 1) * sine[i : i + 1]
        high = rounded(turned)
        whole.append(jnp.where(qlane < 64, high, turned - high))
    message[0 : 2 * queries, :] = jnp.concatenate(whole, axis=0).astype(BF)

    latent = new_latent[:, :kvl].astype(F32)
    square = jnp.mean(latent * latent, axis=-1, keepdims=True)
    gains = gain[...].astype(F32)
    gains = jnp.concatenate([gains[c : c + 1] for c in range(kvl // LANES)], axis=1)
    new_c = rounded(latent * lax.rsqrt(square + EPS) * gains)
    key = doubled(new_latent[:, kvl:].astype(F32))
    key = key * cosine + pltpu.roll(key, 32, 1) * sine
    home[...] = jnp.zeros_like(home)
    home[0:rows, 0:kvl] = new_c
    home[0:rows, kvl : kvl + LANES] = key
    meta[...] = jnp.zeros_like(meta)
    for c in range(kvl // LANES):
        meta[rows * (NEW + c) : rows * (NEW + c + 1), :] = new_c[:, c * LANES : (c + 1) * LANES]
    c = kvl // LANES
    meta[rows * (NEW + c) : rows * (NEW + c + 1), :] = key

    one = lane_ids((1, LANES))
    for i in range(rows):
        length = lengths[i]
        slot = new_slot[i]
        tail = table[i, length // 64]
        for n, value in ((TAIL_LEN, length % 64), (DEST, slot // rows), (DEST_SLOT, slot % rows)):
            at = rows * n + i
            meta[at : at + 1, :] = jnp.full((1, LANES), value, jnp.int32).astype(F32)
        counts = [jnp.zeros((1, LANES), jnp.int32) for _ in range(wide)]
        for j in range(maxblk):
            block = table[i, j]
            count = jnp.clip(length - 64 * j, 0, 64)
            for w in range(wide):
                counts[w] = counts[w] + jnp.where(one + w * LANES == block, count, 0)
        for w in range(wide):
            at = rows * (COUNT + w) + i
            meta[at : at + 1, :] = counts[w].astype(F32)
            at = rows * (COUNT + wide + w) + i
            meta[at : at + 1, :] = jnp.where(one + w * LANES == tail, 1.0, 0.0)
    message[2 * queries : 2 * queries + META, :] = meta[...].astype(BF)


def attend_kernel(owners, head_parts, rows, heads, *refs):
    messages = refs[:owners]
    home, w_uk, pool, w_uv_hbm = refs[owners : owners + 4]
    replies = refs[owners + 4 : 2 * owners + 4]
    w_uv, q_flat, lat, scores, weights, out, each, bias, tops, totals, new_scores, sems = refs[
        2 * owners + 4 :
    ]
    w_uv_copies = copies_of([w_uv_hbm], [w_uv], sems, 1)
    slots, block, width = pool.shape
    tokens = slots * block
    kvl = w_uk.shape[2]
    tiles = kvl // LANES
    queries = rows * heads
    everyone = owners * rows
    wide = (owners * slots + LANES - 1) // LANES
    me = lax.axis_index("pool")
    part = lax.axis_index(("head", "sub"))

    for k in range(owners):
        q_flat[k * queries : (k + 1) * queries, :] = messages[k][0:queries, :].astype(F32)
        told = messages[k][2 * queries : 2 * queries + META, :].astype(F32)
        for n in range(each.shape[0]):
            each[n, rows * k : rows * (k + 1), :] = told[rows * n : rows * (n + 1), :]

    def absorb(h):
        one_head = q_flat[pl.ds(h, everyone, stride=heads), :].astype(BF)
        absorbed = jnp.dot(one_head, w_uk[h], preferred_element_type=F32)
        for c in range(tiles):
            lat[c, pl.ds(h, everyone, stride=heads), :] = absorbed[:, c * LANES : (c + 1) * LANES]

    each_of(heads, ABSORB_UNROLL, absorb)

    lane = lane_ids((LANES, tokens))
    counts = jnp.zeros((everyone, tokens), F32)
    for w in range(wide):
        here = jnp.where(
            row_ids((LANES, tokens)) + w * LANES == me * slots + lane // block, 1.0, 0.0
        ).astype(BF)
        counts = counts + jnp.dot(each[COUNT + w].astype(BF), here, preferred_element_type=F32)
    within = (lane_ids((everyone, tokens)) % block).astype(F32)
    bias[...] = jnp.where(within < counts, 0.0, NONE)

    turned = jnp.concatenate(
        [messages[k][queries : 2 * queries, :] for k in range(owners)], axis=0
    )
    flat_pool = pool[...].reshape(tokens, width)
    full = jnp.concatenate([lat[c].astype(BF) for c in range(tiles)] + [turned], axis=1)
    keys = jnp.concatenate([flat_pool, flat_pool[:, kvl:]], axis=1)
    scores[...] = lax.dot_general(
        full, keys, (((1,), (1,)), ((), ())), preferred_element_type=F32
    )

    new_score = jnp.zeros((queries, LANES), F32)
    new_c = []
    for c in range(tiles):
        new_c.append(
            jnp.concatenate(
                [
                    jnp.broadcast_to(
                        home[r : r + 1, c * LANES : (c + 1) * LANES], (heads, LANES)
                    )
                    for r in range(rows)
                ],
                axis=0,
            )
        )
        new_score = new_score + rounded(lat[c, 0:queries, :]) * new_c[c]
    both = messages[0][queries : 2 * queries, :].astype(F32)
    both = both + pltpu.roll(both, 64, 1)
    new_key = jnp.concatenate(
        [
            jnp.broadcast_to(home[r : r + 1, kvl : kvl + LANES], (heads, LANES))
            for r in range(rows)
        ],
        axis=0,
    )
    new_score = new_score + 0.5 * both * new_key
    new_score = jnp.sum(new_score, axis=1, keepdims=True) * (SCALE * LOG2E)
    new_scores[...] = jnp.full(new_scores.shape, NONE, F32)
    new_scores[0:queries, :] = jnp.broadcast_to(new_score, (queries, LANES))

    chunk = 16

    def soften(n):
        at = pl.ds(pl.multiple_of(n * chunk, chunk), chunk)
        if heads >= chunk:
            shown = bias[pl.ds(n * chunk // heads, 1), :]
        else:
            shown = [bias[pl.ds(n * (chunk // heads) + m, 1), :] for m in range(chunk // heads)]
            shown = [jnp.broadcast_to(one, (heads, tokens)) for one in shown]
            shown = jnp.concatenate(shown, axis=0)
        some = scores[at, :] * (SCALE * LOG2E) + shown
        new = new_scores[at, 0:1]
        top = jnp.maximum(jnp.max(some, axis=1, keepdims=True), new)
        weight = jnp.exp2(some - top).astype(BF)
        weights[at, :] = weight
        total = jnp.sum(weight.astype(F32), axis=1, keepdims=True)
        total = jnp.where(top > 0.5 * NONE, total + rounded(jnp.exp2(new - top)), 0.0)
        tops[at, :] = jnp.broadcast_to(top, (chunk, LANES))
        totals[at, :] = jnp.broadcast_to(total, (chunk, LANES))

    each_of(owners * queries // chunk, SOFTEN_UNROLL, soften)
    sums = jnp.dot(weights[...], flat_pool[:, :kvl], preferred_element_type=F32)
    share = jnp.where(totals[...] > 0.0, 1.0 / jnp.maximum(totals[...], 1e-30), 0.0)
    new_weight = rounded(jnp.exp2(new_scores[0:queries, :] - tops[0:queries, :]))
    for c in range(tiles):
        some = sums[:, c * LANES : (c + 1) * LANES]
        lat[c, 0:queries, :] = (some[0:queries] + new_weight * new_c[c]) * share[0:queries]
        lat[c, queries:, :] = some[queries:] * share[queries:]

    for copy in w_uv_copies:
        copy.wait()

    def project(h):
        one_head = jnp.concatenate(
            [lat[c, pl.ds(h, everyone, stride=heads), :] for c in range(tiles)], axis=1
        ).astype(BF)
        out[pl.ds(h, everyone, stride=heads), :] = jnp.dot(
            one_head, w_uv[h], preferred_element_type=F32
        )

    each_of(heads, PROJECT_UNROLL, project)

    span = block // head_parts
    tails = everyone * span
    if span % 16 == 0:
        near_span, first = span, part * span
        near_pool = pool[:, pl.ds(pl.multiple_of(first, span), span), :]
        near_pool = near_pool.reshape(slots * span, width)
    else:
        near_span, first = block, 0
        near_pool = flat_pool
    near = slots * near_span
    dest = (each[DEST].astype(jnp.int32) ^ me) * rows + each[DEST_SLOT].astype(jnp.int32)
    dest = jnp.concatenate([dest] * (tails // LANES), axis=1)
    goes = jnp.where(dest == lane_ids((everyone, tails)) // span, 1.0, 0.0).astype(BF)
    facts = [each[COUNT + wide + w] for w in range(wide)] + [each[TAIL_LEN]]
    facts = jnp.concatenate(facts + [each[NEW + c] for c in range(tiles + 1)], axis=1).astype(BF)
    facts = lax.dot_general(goes, facts, (((0,), (0,)), ((), ())), preferred_element_type=F32)
    is_last = facts[:, 0 : wide * LANES].astype(BF)
    tail_len = facts[:, wide * LANES : (wide + 1) * LANES]
    new_rows = facts[:, (wide + 1) * LANES :]
    pool_row = row_ids((wide * LANES, near + LANES)) - me * slots
    pool_lane = lane_ids((wide * LANES, near + LANES))
    here = (pool_row == pool_lane // near_span) & (pool_lane < near)
    here = here | ((pool_lane >= near) & (pool_row >= 0) & (pool_row < slots))
    chosen = jnp.dot(
        is_last, jnp.where(here, 1.0, 0.0).astype(BF), preferred_element_type=F32
    )
    is_holder = chosen[:, near:] > 0.5
    token = (part * span + row_ids((tails, LANES)) % span).astype(F32)
    place = row_ids((tails, near))
    diagonal = part * span + place % span == first + lane_ids((tails, near)) % near_span
    is_old = jnp.concatenate([token < tail_len] * (near // LANES), axis=1)
    chosen = jnp.where(diagonal & is_old, chosen[:, :near], 0.0).astype(BF)
    tail_rows = jnp.dot(chosen, near_pool, preferred_element_type=F32)
    tail_rows = jnp.concatenate([tail_rows, tail_rows[:, kvl:]], axis=1)
    is_new = is_holder & (token == tail_len)

    lane = lane_ids((heads, LANES))
    tail_lane = lane_ids((rows * span, LANES))
    for k in range(owners):
        mine = slice(k * rows * span, (k + 1) * rows * span)
        whole = [out[k * queries : (k + 1) * queries, :]]
        for c in range(tiles + 1):
            at = slice(c * LANES, (c + 1) * LANES)
            whole.append(tail_rows[mine, at] + jnp.where(is_new[mine], new_rows[mine, at], 0.0))
        stats = jnp.zeros((heads, LANES), F32)
        for i in range(rows):
            r = k * rows + i
            total = totals[r * heads : (r + 1) * heads, :]
            value = tops[r * heads : (r + 1) * heads, :] + jnp.log2(jnp.maximum(total, 1e-30))
            value = jnp.where(total > 0.0, value, NONE)
            for piece in range(3):
                high = rounded(value)
                stats = jnp.where(lane == 64 + 3 * i + piece, high, stats)
                value = value - high
        whole[-1] = jnp.where(tail_lane < 64, whole[-1], stats)
        whole = jnp.concatenate(whole, axis=0)
        missing = replies[k].shape[0] - whole.shape[0]
        if missing:
            whole = jnp.concatenate([whole, jnp.zeros((missing, LANES), F32)], axis=0)
        replies[k][...] = whole.astype(BF)


def combine_kernel(rows, heads, span, *refs):
    replies = [reply[...].astype(F32) for reply in refs[:-2]]
    attn_out, new_blocks = refs[-2:]
    kvl_tiles = new_blocks.shape[2] // LANES
    queries = rows * heads
    last = queries + kvl_tiles * rows * span
    stats = [reply[last : last + heads, :] for reply in replies]
    for i in range(rows):
        at = 64 + 3 * i
        sizes = [
            stat[:, at : at + 1] + stat[:, at + 1 : at + 2] + stat[:, at + 2 : at + 3]
            for stat in stats
        ]
        top = functools.reduce(jnp.maximum, sizes)
        shares = [jnp.exp2(size - top) for size in sizes]
        denominator = functools.reduce(jnp.add, shares)
        result = jnp.zeros((heads, LANES), F32)
        for share, reply in zip(shares, replies):
            result = result + share * reply[i * heads : (i + 1) * heads, :]
        attn_out[i] = (result / denominator).astype(BF)
    for c in range(kvl_tiles + 1):
        at = queries + c * rows * span
        tile = replies[0][at : at + rows * span, :]
        for reply in replies[1:]:
            tile = tile + reply[at : at + rows * span, :]
        left = min(LANES, new_blocks.shape[2] - c * LANES)
        for i in range(rows):
            new_blocks[i, :, c * LANES : c * LANES + left] = tile[
                i * span : (i + 1) * span, 0:left
            ].astype(BF)


def swap_order(owners):
    steps = list(range(1, owners))
    return [k for k in steps if k % 2] + [k for k in steps if k % 2 == 0]


def per_device(
    pool, block_table, lengths, new_slot, q_nope, q_rope, new_latent, kv_gain, w_uk, w_uv
):
    owners = lax.axis_size("pool")
    parts = lax.axis_size(("head", "sub"))
    slots, block, width = pool.shape
    rows, heads, nope = q_nope.shape
    rope = q_rope.shape[2]
    kvl = kv_gain.shape[0]
    vdim = w_uv.shape[2]
    queries = rows * heads
    everyone = owners * rows
    wide = (owners * slots + LANES - 1) // LANES
    span = block // parts
    tokens = slots * block
    vmem = pl.BlockSpec(memory_space=pltpu.VMEM)
    hbm = pl.BlockSpec(memory_space=pltpu.HBM)

    half = rope // 2
    freq = 10000.0 ** (-(np.arange(LANES) % half).astype(np.float32) / np.float32(half))
    freq = jnp.asarray(freq.astype(np.float32)[None])
    gain = kv_gain.reshape(-1, LANES)
    raw = (block_table, lengths, new_slot, q_nope, q_rope, new_latent, gain, freq)
    raw = [pltpu.with_memory_space_constraint(a, pltpu.HBM) for a in raw]
    message, home = pl.pallas_call(
        functools.partial(query_kernel, wide),
        out_shape=(
            pltpu.VMEM((2 * queries + META, LANES), BF),
            pltpu.VMEM((8, kvl + LANES), F32),
        ),
        in_specs=[hbm] * len(raw),
        out_specs=(vmem, vmem),
        scratch_shapes=[
            (pltpu.SMEM if n < 3 else pltpu.VMEM)(a.shape, a.dtype) for n, a in enumerate(raw)
        ]
        + [pltpu.VMEM((META, LANES), F32), pltpu.SemaphoreType.DMA((len(raw),))],
        compiler_params=pltpu.CompilerParams(vmem_limit_bytes=4 * 2**20),
        name="queries",
    )(*raw)

    def swap(array, k):
        return lax.ppermute(array, "pool", [(i, i ^ k) for i in range(owners)])

    order = swap_order(owners)
    messages = [message] + [None] * (owners - 1)
    for k in order:
        messages[k] = swap(message, k)

    pool, w_uk, w_uv = [
        pltpu.with_memory_space_constraint(a, pltpu.HBM) for a in (pool, w_uk, w_uv)
    ]
    w_uk, pool = pl.pallas_call(
        load_kernel,
        out_shape=(pltpu.VMEM(w_uk.shape, BF), pltpu.VMEM(pool.shape, BF)),
        in_specs=[hbm] * 2,
        out_specs=(vmem, vmem),
        scratch_shapes=[pltpu.SemaphoreType.DMA((8,))],
        compiler_params=pltpu.CompilerParams(vmem_limit_bytes=2**20),
        cost_estimate=pl.CostEstimate(flops=0, bytes_accessed=20 * 2**20, transcendentals=0),
        name="load",
    )(w_uk, pool)

    reply_rows = -(-(queries + (kvl // LANES + 1) * rows * span) // 16) * 16
    replies = pl.pallas_call(
        functools.partial(attend_kernel, owners, parts, rows, heads),
        out_shape=tuple(
            jax.ShapeDtypeStruct((reply_rows, LANES), BF) for _ in range(owners)
        ),
        in_specs=[vmem] * (owners + 3) + [hbm],
        out_specs=tuple([vmem] * owners),
        scratch_shapes=[
            pltpu.VMEM(w_uv.shape, BF),
            pltpu.VMEM((owners * queries, nope), F32),
            pltpu.VMEM((kvl // LANES, owners * queries, LANES), F32),
            pltpu.VMEM((owners * queries, tokens), F32),
            pltpu.VMEM((owners * queries, tokens), BF),
            pltpu.VMEM((owners * queries, vdim), F32),
            pltpu.VMEM((COUNT + 2 * wide, everyone, LANES), F32),
            pltpu.VMEM((everyone, tokens), F32),
            pltpu.VMEM((owners * queries, LANES), F32),
            pltpu.VMEM((owners * queries, LANES), F32),
            pltpu.VMEM((owners * queries, LANES), F32),
            pltpu.SemaphoreType.DMA((1,)),
        ],
        compiler_params=pltpu.CompilerParams(vmem_limit_bytes=24 * 2**20),
        name="attend",
    )(*messages, home, w_uk, pool, w_uv)

    returned = [replies[0]] + [None] * (owners - 1)
    for k in order:
        returned[k] = swap(replies[k], k)

    return pl.pallas_call(
        functools.partial(combine_kernel, rows, heads, span),
        out_shape=(
            jax.ShapeDtypeStruct((rows, heads, vdim), BF),
            jax.ShapeDtypeStruct((rows, span, width), BF),
        ),
        in_specs=[vmem] * owners,
        out_specs=(vmem, vmem),
        compiler_params=pltpu.CompilerParams(vmem_limit_bytes=4 * 2**20),
        name="combine",
    )(*returned)


def solution(mesh):
    placed = (
        P(("grp", "pool"), None, None),
        P(("grp", "pool"), None),
        P(("grp", "pool")),
        P(("grp", "pool")),
        P(("grp", "pool"), ("head", "sub"), None),
        P(("grp", "pool"), ("head", "sub"), None),
        P(("grp", "pool"), None),
        P(),
        P(("head", "sub"), None, None),
        P(("head", "sub"), None, None),
    )
    return jax.shard_map(
        per_device,
        mesh=mesh,
        in_specs=placed,
        out_specs=(
            P(("grp", "pool"), ("head", "sub"), None),
            P(("grp", "pool"), ("head", "sub"), None),
        ),
        check_vma=False,
    )
```

time: 27 us -> 25.6 us (0.948)
  Pallas kernels: 10.1 us -> 8.67 us
  starting transfers between devices: 9.42 us -> 10.2 us
  waiting for transfers between devices: 6.68 us -> 5.9 us
    pallas_call x1, Pallas kernels: 4.06 us -> 2.8 us  [per_device(): pl.pallas_call(load_kernel, out_shape=(pltpu.VMEM(w_uk.shape, BF), pltpu....]
    ppermute x6, starting transfers between devices: 9.42 us -> 10.2 us  [swap(): return lax.ppermute(array, 'pool', [(i, i ^ k) for i in range(owners)])]
    ppermute x6, waiting for transfers between devices: 6.68 us -> 5.9 us  [swap(): return lax.ppermute(array, 'pool', [(i, i ^ k) for i in range(owners)])]
  transfers between devices with their start and end apart: 6 -> 6, of which waited for: 4 -> 3; matrix products, arithmetic and copies ran while one was open for 0% -> 0% of each run, Pallas kernels for 15% -> 11%
where the time goes in v2:
time: 25.6 us; the launch traced here: 25.5 us
  starting transfers between devices  10.2 us (40%)
  Pallas kernels  8.67 us (34%)
  waiting for transfers between devices  5.9 us (23%)
  between operations  0.67 us (3%)
    ppermute x6, starting transfers between devices, swap(): return lax.ppermute(array, 'pool', [(i, i ^ k) for i in range(owners)])  10.2 us
    ppermute x6, waiting for transfers between devices, swap(): return lax.ppermute(array, 'pool', [(i, i ^ k) for i in range(owners)])  5.9 us
    pallas_call x1, Pallas kernels, per_device(): pl.pallas_call(functools.partial(attend_kernel, owners, parts, rows, head...  4.05 us
    pallas_call x1, Pallas kernels, per_device(): pl.pallas_call(load_kernel, out_shape=(pltpu.VMEM(w_uk.shape, BF), pltpu....  2.8 us
    pallas_call x1, Pallas kernels, per_device(): pl.pallas_call(functools.partial(query_kernel, wide), out_shape=(pltpu.VM...  1.01 us
    pallas_call x1, Pallas kernels, per_device(): pl.pallas_call(functools.partial(combine_kernel, rows, heads, span), out_...  0.82 us
  transfers between devices with their start and end apart: 6, of which 3 were waited for; matrix products, arithmetic and copies ran while one was open for 0% of the time, Pallas kernels for 11%

profile of v2, /device:TPU:0, one launch (start us, length us, event | category | flops | bytes accessed | tf_op | source)
XLA Modules:
  0.0 25.5 jit_solution(16678116894386493619)
XLA Ops:
  0.6 1.0 %queries.1 = (bf16[160,128]{1,0:T(8,128)(2,1)S(1)}, f32[8,640]{1,0:T(8,128)S(1)}) custom-call(s32[2,32]{1,0:T(2,128)} %refs_0_.1, s32[2]{0:T(128)} %refs_1_.1, s32[2]{0:T(128)} %refs_2_.1, bf16[2,32,128]{2,1,0:T(8,128)(2,1)} %refs_3_.1, bf16[2,32,64]{2,1,0:T(8,128)(2,1)} %refs_4_.1, bf16[2,576]{1,0:T(2,128)(2,1)} %refs_5_.1, bf16[4,128]{1,0:T(4,128)(2,1)} %bitcast.1, ...), custom_call_target="tpu_custom_call" | custom-call | tf_op jit(solution)/shard_map/queries/pallas_call | solution.py:389
  1.7 5.1 %collective-permute-start.2 = (bf16[160,128]{1,0:T(8,128)(2,1)S(1)}, bf16[160,128]{1,0:T(8,128)(2,1)S(1)}, u32[]{:S(2)}, u32[]{:S(2)}) collective-permute-start(bf16[160,128]{1,0:T(8,128)(2,1)S(1)} %get-tuple-element.10.refs_0_), channel_id=1, source_target_pairs={{0,12},{4,8},{8,4},{12,0},{1,13},{5,9},{9,5},{13,1},{2,14},{6,10},... | collective-permute-start | bytes 122888 | tf_op jit(solution)/shard_map/ppermute | solution.py:406
  6.8 0.0 collective-permute-start.1
  6.8 0.6 %collective-permute-start = (bf16[160,128]{1,0:T(8,128)(2,1)S(1)}, bf16[160,128]{1,0:T(8,128)(2,1)S(1)}, u32[]{:S(2)}, u32[]{:S(2)}) collective-permute-start(bf16[160,128]{1,0:T(8,128)(2,1)S(1)} %get-tuple-element.10.refs_0_), channel_id=1, source_target_pairs={{0,4},{4,0},{8,12},{12,8},{1,5},{5,1},{9,13},{13,9},{2,6},{6,2},{1... | collective-permute-start | bytes 122888 | tf_op jit(solution)/shard_map/ppermute | solution.py:406
  7.4 2.8 %load.1 = (bf16[32,128,512]{2,1,0:T(8,128)(2,1)S(1)}, bf16[24,64,576]{2,1,0:T(8,128)(2,1)S(1)}) custom-call(bf16[32,128,512]{2,1,0:T(8,128)(2,1)} %w_uk_hbm.1, bf16[24,64,576]{2,1,0:T(8,128)(2,1)} %pool_hbm.1), custom_call_target="tpu_custom_call" | custom-call | bytes 20971520 | tf_op jit(solution)/shard_map/load/pallas_call | solution.py:416
  10.2 0.0 collective-permute-done.2.refs_3_
  10.2 1.4 %collective-permute-done.1.refs_2_ = bf16[160,128]{1,0:T(8,128)(2,1)S(1)} collective-permute-done((bf16[160,128]{1,0:T(8,128)(2,1)S(1)}, bf16[160,128]{1,0:T(8,128)(2,1)S(1)}, u32[]{:S(2)}, u32[]{:S(2)}) %collective-permute-start.1) | collective-permute-done | bytes 40992 | tf_op jit(solution)/shard_map/ppermute | solution.py:406
  11.7 0.0 collective-permute-done.refs_1_
  11.7 4.0 %attend.1 = (bf16[224,128]{1,0:T(8,128)(2,1)S(1)}, bf16[224,128]{1,0:T(8,128)(2,1)S(1)}, bf16[224,128]{1,0:T(8,128)(2,1)S(1)}, bf16[224,128]{1,0:T(8,128)(2,1)S(1)}) custom-call(bf16[160,128]{1,0:T(8,128)(2,1)S(1)} %get-tuple-element.10.refs_0_, bf16[160,128]{1,0:T(8,128)(2,1)S(1)} %collective-permute-done.refs_1_, ...), custom_call_target="tpu_custom_call" | custom-call | tf_op jit(solution)/shard_map/attend/pallas_call | solution.py:428
  15.7 0.2 collective-permute-start.3
  16.0 2.7 %collective-permute-start.4 = (bf16[224,128]{1,0:T(8,128)(2,1)S(1)}, bf16[224,128]{1,0:T(8,128)(2,1)S(1)}, u32[]{:S(2)}, u32[]{:S(2)}) collective-permute-start(bf16[224,128]{1,0:T(8,128)(2,1)S(1)} %get-tuple-element.16), channel_id=1, source_target_pairs={{0,8},{4,12},{8,0},{12,4},{1,9},{5,13},{9,1},{13,5},{2,10},{6,14},... | collective-permute-start | bytes 172040 | tf_op jit(solution)/shard_map/ppermute | solution.py:406
  18.7 1.5 %collective-permute-start.5 = (bf16[224,128]{1,0:T(8,128)(2,1)S(1)}, bf16[224,128]{1,0:T(8,128)(2,1)S(1)}, u32[]{:S(2)}, u32[]{:S(2)}) collective-permute-start(bf16[224,128]{1,0:T(8,128)(2,1)S(1)} %get-tuple-element.17), channel_id=1, source_target_pairs={{0,12},{4,8},{8,4},{12,0},{1,13},{5,9},{9,5},{13,1},{2,14},{6,10},... | collective-permute-start | bytes 172040 | tf_op jit(solution)/shard_map/ppermute | solution.py:406
  20.2 0.0 collective-permute-done.3.refs_1_
  20.2 0.8 %collective-permute-done.4.refs_2_ = bf16[224,128]{1,0:T(8,128)(2,1)S(1)} collective-permute-done((bf16[224,128]{1,0:T(8,128)(2,1)S(1)}, bf16[224,128]{1,0:T(8,128)(2,1)S(1)}, u32[]{:S(2)}, u32[]{:S(2)}) %collective-permute-start.4) | collective-permute-done | bytes 57376 | tf_op jit(solution)/shard_map/ppermute | solution.py:406
  21.0 3.6 %collective-permute-done.5.refs_3_ = bf16[224,128]{1,0:T(8,128)(2,1)S(1)} collective-permute-done((bf16[224,128]{1,0:T(8,128)(2,1)S(1)}, bf16[224,128]{1,0:T(8,128)(2,1)S(1)}, u32[]{:S(2)}, u32[]{:S(2)}) %collective-permute-start.5) | collective-permute-done | bytes 57376 | tf_op jit(solution)/shard_map/ppermute | solution.py:406
  24.6 0.8 %combine.1 = (bf16[2,32,128]{2,1,0:T(8,128)(2,1)}, bf16[2,16,576]{2,1,0:T(8,128)(2,1)}) custom-call(bf16[224,128]{1,0:T(8,128)(2,1)S(1)} %get-tuple-element.14.refs_0_, bf16[224,128]{1,0:T(8,128)(2,1)S(1)} %collective-permute-done.3.refs_1_, bf16[224,128]{1,0:T(8,128)(2,1)S(1)} %collective-permute-done.4.refs_2_, ...), custom_call_target="tpu_custom_call" | custom-call | tf_op jit(solution)/shard_map/combine/pallas_call | solution.py:457
Async XLA Ops:
  1.7 8.6 %collective-permute-start.2 = (bf16[160,128]{1,0:T(8,128)(2,1)S(1)}, bf16[160,128]{1,0:T(8,128)(2,1)S(1)}, u32[]{:S(2)}, u32[]{:S(2)}) collective-permute-start(bf16[160,128]{1,0:T(8,128)(2,1)S(1)} %get-tuple-element.10.refs_0_), channel_id=1, source_target_pairs={{0,12},{4,8},{8,4},{12,0},{1,13},{5,9},{9,5},{13,1},{2,14},{6,10},... | collective-permute-start | bytes 122888 | tf_op jit(solution)/shard_map/ppermute | solution.py:406
  6.8 4.9 %collective-permute-start.1 = (bf16[160,128]{1,0:T(8,128)(2,1)S(1)}, bf16[160,128]{1,0:T(8,128)(2,1)S(1)}, u32[]{:S(2)}, u32[]{:S(2)}) collective-permute-start(bf16[160,128]{1,0:T(8,128)(2,1)S(1)} %get-tuple-element.10.refs_0_), channel_id=1, source_target_pairs={{0,8},{4,12},{8,0},{12,4},{1,9},{5,13},{9,1},{13,5},{2,10},{6,14},... | collective-permute-start | bytes 122888 | tf_op jit(solution)/shard_map/ppermute | solution.py:406
  6.8 4.9 %collective-permute-start = (bf16[160,128]{1,0:T(8,128)(2,1)S(1)}, bf16[160,128]{1,0:T(8,128)(2,1)S(1)}, u32[]{:S(2)}, u32[]{:S(2)}) collective-permute-start(bf16[160,128]{1,0:T(8,128)(2,1)S(1)} %get-tuple-element.10.refs_0_), channel_id=1, source_target_pairs={{0,4},{4,0},{8,12},{12,8},{1,5},{5,1},{9,13},{13,9},{2,6},{6,2},{1... | collective-permute-start | bytes 122888 | tf_op jit(solution)/shard_map/ppermute | solution.py:406
  15.7 4.5 %collective-permute-start.3 = (bf16[224,128]{1,0:T(8,128)(2,1)S(1)}, bf16[224,128]{1,0:T(8,128)(2,1)S(1)}, u32[]{:S(2)}, u32[]{:S(2)}) collective-permute-start(bf16[224,128]{1,0:T(8,128)(2,1)S(1)} %get-tuple-element.15), channel_id=1, source_target_pairs={{0,4},{4,0},{8,12},{12,8},{1,5},{5,1},{9,13},{13,9},{2,6},{6,2},{1... | collective-permute-start | bytes 172040 | tf_op jit(solution)/shard_map/ppermute | solution.py:406
  16.0 5.1 %collective-permute-start.4 = (bf16[224,128]{1,0:T(8,128)(2,1)S(1)}, bf16[224,128]{1,0:T(8,128)(2,1)S(1)}, u32[]{:S(2)}, u32[]{:S(2)}) collective-permute-start(bf16[224,128]{1,0:T(8,128)(2,1)S(1)} %get-tuple-element.16), channel_id=1, source_target_pairs={{0,8},{4,12},{8,0},{12,4},{1,9},{5,13},{9,1},{13,5},{2,10},{6,14},... | collective-permute-start | bytes 172040 | tf_op jit(solution)/shard_map/ppermute | solution.py:406
  18.7 6.0 %collective-permute-start.5 = (bf16[224,128]{1,0:T(8,128)(2,1)S(1)}, bf16[224,128]{1,0:T(8,128)(2,1)S(1)}, u32[]{:S(2)}, u32[]{:S(2)}) collective-permute-start(bf16[224,128]{1,0:T(8,128)(2,1)S(1)} %get-tuple-element.17), channel_id=1, source_target_pairs={{0,12},{4,8},{8,4},{12,0},{1,13},{5,9},{9,5},{13,1},{2,14},{6,10},... | collective-permute-start | bytes 172040 | tf_op jit(solution)/shard_map/ppermute | solution.py:406

commit v3 on v2

--- a/solution.py
+++ b/solution.py
@@ -49,6 +49,11 @@
             return carry
 
         lax.fori_loop(0, count // unroll, some, 0)
+
+
+def near_span(block, head_parts):
+    span = block // head_parts
+    return span if span % 16 == 0 else block
 
 
 def copies_of(sources, targets, sems, pieces=1):
@@ -65,8 +70,27 @@
     return copies
 
 
-def load_kernel(w_uk_hbm, pool_hbm, w_uk, pool, sems):
-    for copy in copies_of([w_uk_hbm, pool_hbm], [w_uk, pool], sems, 4):
+def load_kernel(head_parts, w_uk_hbm, pool_hbm, w_uk, keys, row_place, tail_place, pool, sems):
+    copies = copies_of([pool_hbm, w_uk_hbm], [pool, w_uk], sems, 4)
+    slots, block, width = pool.shape
+    kvl = w_uk.shape[2]
+    me = lax.axis_index("pool")
+
+    owned = row_ids(row_place.shape) - me * slots
+    row_place[...] = jnp.where(owned == lane_ids(row_place.shape) // block, 1.0, 0.0).astype(BF)
+    span = near_span(block, head_parts)
+    near = slots * span
+    owned = row_ids(tail_place.shape) - me * slots
+    lane = lane_ids(tail_place.shape)
+    here = (owned == lane // span) & (lane < near)
+    here = here | ((lane >= near) & (owned >= 0) & (owned < slots))
+    tail_place[...] = jnp.where(here, 1.0, 0.0).astype(BF)
+
+    for copy in copies[:4]:
+        copy.wait()
+    keys[:, :, 0:kvl] = pool[:, :, 0:kvl]
+    keys[:, :, kvl:] = doubled(pool[:, :, kvl:])
+    for copy in copies[4:]:
         copy.wait()
 
 
@@ -141,11 +165,11 @@
 
 
 def attend_kernel(owners, head_parts, rows, heads, *refs):
-    messages = refs[:owners]
-    home, w_uk, pool, w_uv_hbm = refs[owners : owners + 4]
-    replies = refs[owners + 4 : 2 * owners + 4]
+    messages = [refs[operand_orders(owners)[0].index(k)] for k in range(owners)]
+    home, w_uk, pool, row_place, tail_place, w_uv_hbm = refs[owners : owners + 6]
+    replies = refs[owners + 6 : 2 * owners + 6]
     w_uv, q_flat, lat, scores, weights, out, each, bias, tops, totals, new_scores, sems = refs[
-        2 * owners + 4 :
+        2 * owners + 6 :
     ]
     w_uv_copies = copies_of([w_uv_hbm], [w_uv], sems, 1)
     slots, block, width = pool.shape
@@ -172,13 +196,8 @@
 
     each_of(heads, ABSORB_UNROLL, absorb)
 
-    lane = lane_ids((LANES, tokens))
-    counts = jnp.zeros((everyone, tokens), F32)
-    for w in range(wide):
-        here = jnp.where(
-            row_ids((LANES, tokens)) + w * LANES == me * slots + lane // block, 1.0, 0.0
-        ).astype(BF)
-        counts = counts + jnp.dot(each[COUNT + w].astype(BF), here, preferred_element_type=F32)
+    counts = jnp.concatenate([each[COUNT + w] for w in range(wide)], axis=1).astype(BF)
+    counts = jnp.dot(counts, row_place[...], preferred_element_type=F32)
     within = (lane_ids((everyone, tokens)) % block).astype(F32)
     bias[...] = jnp.where(within < counts, 0.0, NONE)
 
@@ -187,10 +206,38 @@
     )
     flat_pool = pool[...].reshape(tokens, width)
     full = jnp.concatenate([lat[c].astype(BF) for c in range(tiles)] + [turned], axis=1)
-    keys = jnp.concatenate([flat_pool, flat_pool[:, kvl:]], axis=1)
     scores[...] = lax.dot_general(
-        full, keys, (((1,), (1,)), ((), ())), preferred_element_type=F32
+        full, flat_pool, (((1,), (1,)), ((), ())), preferred_element_type=F32
     )
+
+    span = block // head_parts
+    tails = everyone * span
+    reach = near_span(block, head_parts)
+    near = slots * reach
+    if reach == span:
+        first = part * span
+        near_pool = pool[:, pl.ds(pl.multiple_of(first, span), span), :].reshape(near, width)
+    else:
+        first = 0
+        near_pool = flat_pool
+    dest = (each[DEST].astype(jnp.int32) ^ me) * rows + each[DEST_SLOT].astype(jnp.int32)
+    dest = jnp.concatenate([dest] * (tails // LANES), axis=1)
+    goes = jnp.where(dest == lane_ids((everyone, tails)) // span, 1.0, 0.0).astype(BF)
+    facts = [each[COUNT + wide + w] for w in range(wide)] + [each[TAIL_LEN]]
+    facts = jnp.concatenate(facts + [each[NEW + c] for c in range(tiles + 1)], axis=1).astype(BF)
+    facts = lax.dot_general(goes, facts, (((0,), (0,)), ((), ())), preferred_element_type=F32)
+    is_last = facts[:, 0 : wide * LANES].astype(BF)
+    tail_len = facts[:, wide * LANES : (wide + 1) * LANES]
+    new_rows = facts[:, (wide + 1) * LANES :]
+    chosen = jnp.dot(is_last, tail_place[...], preferred_element_type=F32)
+    is_holder = chosen[:, near:] > 0.5
+    token = (part * span + row_ids((tails, LANES)) % span).astype(F32)
+    place = row_ids((tails, near))
+    diagonal = part * span + place % span == first + lane_ids((tails, near)) % reach
+    is_old = jnp.concatenate([token < tail_len] * (near // LANES), axis=1)
+    chosen = jnp.where(diagonal & is_old, chosen[:, :near], 0.0).astype(BF)
+    tail_rows = jnp.dot(chosen, near_pool, preferred_element_type=F32)
+    is_new = is_holder & (token == tail_len)
 
     new_score = jnp.zeros((queries, LANES), F32)
     new_c = []
@@ -262,42 +309,6 @@
         )
 
     each_of(heads, PROJECT_UNROLL, project)
-
-    span = block // head_parts
-    tails = everyone * span
-    if span % 16 == 0:
-        near_span, first = span, part * span
-        near_pool = pool[:, pl.ds(pl.multiple_of(first, span), span), :]
-        near_pool = near_pool.reshape(slots * span, width)
-    else:
-        near_span, first = block, 0
-        near_pool = flat_pool
-    near = slots * near_span
-    dest = (each[DEST].astype(jnp.int32) ^ me) * rows + each[DEST_SLOT].astype(jnp.int32)
-    dest = jnp.concatenate([dest] * (tails // LANES), axis=1)
-    goes = jnp.where(dest == lane_ids((everyone, tails)) // span, 1.0, 0.0).astype(BF)
-    facts = [each[COUNT + wide + w] for w in range(wide)] + [each[TAIL_LEN]]
-    facts = jnp.concatenate(facts + [each[NEW + c] for c in range(tiles + 1)], axis=1).astype(BF)
-    facts = lax.dot_general(goes, facts, (((0,), (0,)), ((), ())), preferred_element_type=F32)
-    is_last = facts[:, 0 : wide * LANES].astype(BF)
-    tail_len = facts[:, wide * LANES : (wide + 1) * LANES]
-    new_rows = facts[:, (wide + 1) * LANES :]
-    pool_row = row_ids((wide * LANES, near + LANES)) - me * slots
-    pool_lane = lane_ids((wide * LANES, near + LANES))
-    here = (pool_row == pool_lane // near_span) & (pool_lane < near)
-    here = here | ((pool_lane >= near) & (pool_row >= 0) & (pool_row < slots))
-    chosen = jnp.dot(
-        is_last, jnp.where(here, 1.0, 0.0).astype(BF), preferred_element_type=F32
-    )
-    is_holder = chosen[:, near:] > 0.5
-    token = (part * span + row_ids((tails, LANES)) % span).astype(F32)
-    place = row_ids((tails, near))
-    diagonal = part * span + place % span == first + lane_ids((tails, near)) % near_span
-    is_old = jnp.concatenate([token < tail_len] * (near // LANES), axis=1)
-    chosen = jnp.where(diagonal & is_old, chosen[:, :near], 0.0).astype(BF)
-    tail_rows = jnp.dot(chosen, near_pool, preferred_element_type=F32)
-    tail_rows = jnp.concatenate([tail_rows, tail_rows[:, kvl:]], axis=1)
-    is_new = is_holder & (token == tail_len)
 
     lane = lane_ids((heads, LANES))
     tail_lane = lane_ids((rows * span, LANES))
@@ -357,9 +368,10 @@
             ].astype(BF)
 
 
-def swap_order(owners):
-    steps = list(range(1, owners))
-    return [k for k in steps if k % 2] + [k for k in steps if k % 2 == 0]
+def operand_orders(owners):
+    if owners == 4:
+        return (0, 1, 3, 2), (0, 3, 1, 2)
+    return tuple(range(owners)), tuple(range(owners))
 
 
 def per_device(
@@ -405,21 +417,22 @@
     def swap(array, k):
         return lax.ppermute(array, "pool", [(i, i ^ k) for i in range(owners)])
 
-    order = swap_order(owners)
-    messages = [message] + [None] * (owners - 1)
-    for k in order:
-        messages[k] = swap(message, k)
+    message_order, reply_order = operand_orders(owners)
+    messages = [swap(message, k) if k else message for k in message_order]
 
     pool, w_uk, w_uv = [
         pltpu.with_memory_space_constraint(a, pltpu.HBM) for a in (pool, w_uk, w_uv)
     ]
-    w_uk, pool = pl.pallas_call(
-        load_kernel,
-        out_shape=(pltpu.VMEM(w_uk.shape, BF), pltpu.VMEM(pool.shape, BF)),
+    near = slots * near_span(block, parts)
+    shapes = (w_uk.shape, pool.shape[:2] + (kvl + LANES,))
+    shapes = shapes + ((wide * LANES, tokens), (wide * LANES, near + LANES))
+    loaded = pl.pallas_call(
+        functools.partial(load_kernel, parts),
+        out_shape=tuple(pltpu.VMEM(shape, BF) for shape in shapes),
         in_specs=[hbm] * 2,
-        out_specs=(vmem, vmem),
-        scratch_shapes=[pltpu.SemaphoreType.DMA((8,))],
-        compiler_params=pltpu.CompilerParams(vmem_limit_bytes=2**20),
+        out_specs=(vmem,) * 4,
+        scratch_shapes=[pltpu.VMEM(pool.shape, BF), pltpu.SemaphoreType.DMA((8,))],
+        compiler_params=pltpu.CompilerParams(vmem_limit_bytes=8 * 2**20),
         cost_estimate=pl.CostEstimate(flops=0, bytes_accessed=20 * 2**20, transcendentals=0),
         name="load",
     )(w_uk, pool)
@@ -430,7 +443,7 @@
         out_shape=tuple(
             jax.ShapeDtypeStruct((reply_rows, LANES), BF) for _ in range(owners)
         ),
-        in_specs=[vmem] * (owners + 3) + [hbm],
+        in_specs=[vmem] * (owners + 5) + [hbm],
         out_specs=tuple([vmem] * owners),
         scratch_shapes=[
             pltpu.VMEM(w_uv.shape, BF),
@@ -448,11 +461,9 @@
         ],
         compiler_params=pltpu.CompilerParams(vmem_limit_bytes=24 * 2**20),
         name="attend",
-    )(*messages, home, w_uk, pool, w_uv)
-
-    returned = [replies[0]] + [None] * (owners - 1)
-    for k in order:
-        returned[k] = swap(replies[k], k)
+    )(*messages, home, *loaded, w_uv)
+
+    returned = [swap(replies[k], k) if k else replies[0] for k in reply_order]
 
     return pl.pallas_call(
         functools.partial(combine_kernel, rows, heads, span),

time: 25.6 us -> 23.6 us (0.922)
  waiting for transfers between devices: 5.9 us -> 4.3 us
  Pallas kernels: 8.67 us -> 8.38 us
    ppermute x6, waiting for transfers between devices: 5.9 us -> 4.3 us  [swap(): return lax.ppermute(array, 'pool', [(i, i ^ k) for i in range(owners)])]
    pallas_call x1, Pallas kernels: 4.05 us -> 3.71 us  [per_device(): pl.pallas_call(functools.partial(attend_kernel, owners, parts, rows, head...]
  transfers between devices with their start and end apart: 6 -> 6, of which waited for: 3 -> 3; matrix products, arithmetic and copies ran while one was open for 0% -> 0% of each run, Pallas kernels for 11% -> 12%
where the time goes in v3:
time: 23.6 us; the launch traced here: 23.5 us
  starting transfers between devices  10.1 us (43%)
  Pallas kernels  8.38 us (36%)
  waiting for transfers between devices  4.3 us (18%)
  between operations  0.67 us (3%)
    ppermute x6, starting transfers between devices, swap(): return lax.ppermute(array, 'pool', [(i, i ^ k) for i in range(owners)])  10.1 us
    ppermute x6, waiting for transfers between devices, swap(): return lax.ppermute(array, 'pool', [(i, i ^ k) for i in range(owners)])  4.3 us
    pallas_call x1, Pallas kernels, per_device(): pl.pallas_call(functools.partial(attend_kernel, owners, parts, rows, head...  3.71 us
    pallas_call x1, Pallas kernels, per_device(): pl.pallas_call(functools.partial(load_kernel, parts), out_shape=tuple((pl...  2.84 us
    pallas_call x1, Pallas kernels, per_device(): pl.pallas_call(functools.partial(query_kernel, wide), out_shape=(pltpu.VM...  1.01 us
    pallas_call x1, Pallas kernels, per_device(): pl.pallas_call(functools.partial(combine_kernel, rows, heads, span), out_...  0.82 us
  transfers between devices with their start and end apart: 6, of which 3 were waited for; matrix products, arithmetic and copies ran while one was open for 0% of the time, Pallas kernels for 12%

profile of v3, /device:TPU:0, one launch (start us, length us, event | category | flops | bytes accessed | tf_op | source)
XLA Modules:
  0.0 23.5 jit_solution(16986762135906417037)
XLA Ops:
  0.6 1.0 %queries.1 = (bf16[160,128]{1,0:T(8,128)(2,1)S(1)}, f32[8,640]{1,0:T(8,128)S(1)}) custom-call(s32[2,32]{1,0:T(2,128)} %refs_0_.1, s32[2]{0:T(128)} %refs_1_.1, s32[2]{0:T(128)} %refs_2_.1, bf16[2,32,128]{2,1,0:T(8,128)(2,1)} %refs_3_.1, bf16[2,32,64]{2,1,0:T(8,128)(2,1)} %refs_4_.1, bf16[2,576]{1,0:T(2,128)(2,1)} %refs_5_.1, bf16[4,128]{1,0:T(4,128)(2,1)} %bitcast.1, ...), custom_call_target="tpu_custom_call" | custom-call | tf_op jit(solution)/shard_map/queries/pallas_call | solution.py:401
  1.7 4.1 %collective-permute-start.2 = (bf16[160,128]{1,0:T(8,128)(2,1)S(1)}, bf16[160,128]{1,0:T(8,128)(2,1)S(1)}, u32[]{:S(2)}, u32[]{:S(2)}) collective-permute-start(bf16[160,128]{1,0:T(8,128)(2,1)S(1)} %get-tuple-element.12.refs_0_), channel_id=1, source_target_pairs={{0,8},{4,12},{8,0},{12,4},{1,9},{5,13},{9,1},{13,5},{2,10},{6,14},... | collective-permute-start | bytes 122888 | tf_op jit(solution)/shard_map/ppermute | solution.py:418
  5.8 1.3 %collective-permute-start.1 = (bf16[160,128]{1,0:T(8,128)(2,1)S(1)}, bf16[160,128]{1,0:T(8,128)(2,1)S(1)}, u32[]{:S(2)}, u32[]{:S(2)}) collective-permute-start(bf16[160,128]{1,0:T(8,128)(2,1)S(1)} %get-tuple-element.12.refs_0_), channel_id=1, source_target_pairs={{0,12},{4,8},{8,4},{12,0},{1,13},{5,9},{9,5},{13,1},{2,14},{6,10},... | collective-permute-start | bytes 122888 | tf_op jit(solution)/shard_map/ppermute | solution.py:418
  7.1 0.2 collective-permute-start
  7.3 2.8 %load.1 = (bf16[32,128,512]{2,1,0:T(8,128)(2,1)S(1)}, bf16[24,64,640]{2,1,0:T(8,128)(2,1)S(1)}, bf16[128,1536]{1,0:T(8,128)(2,1)S(1)}, bf16[128,512]{1,0:T(8,128)(2,1)S(1)}) custom-call(bf16[32,128,512]{2,1,0:T(8,128)(2,1)} %w_uk_hbm.1, bf16[24,64,576]{2,1,0:T(8,128)(2,1)} %pool_hbm.1), custom_call_target="tpu_custom_call" | custom-call | bytes 20971520 | tf_op jit(solution)/shard_map/load/pallas_call | solution.py:429
  10.2 0.0 collective-permute-done.2.refs_3_
  10.2 1.4 %collective-permute-done.1.refs_2_ = bf16[160,128]{1,0:T(8,128)(2,1)S(1)} collective-permute-done((bf16[160,128]{1,0:T(8,128)(2,1)S(1)}, bf16[160,128]{1,0:T(8,128)(2,1)S(1)}, u32[]{:S(2)}, u32[]{:S(2)}) %collective-permute-start.1) | collective-permute-done | bytes 40992 | tf_op jit(solution)/shard_map/ppermute | solution.py:418
  11.6 0.0 collective-permute-done.refs_1_
  11.6 3.7 %attend.1 = (bf16[224,128]{1,0:T(8,128)(2,1)S(1)}, bf16[224,128]{1,0:T(8,128)(2,1)S(1)}, bf16[224,128]{1,0:T(8,128)(2,1)S(1)}, bf16[224,128]{1,0:T(8,128)(2,1)S(1)}) custom-call(bf16[160,128]{1,0:T(8,128)(2,1)S(1)} %get-tuple-element.12.refs_0_, bf16[160,128]{1,0:T(8,128)(2,1)S(1)} %collective-permute-done.refs_1_, ...), custom_call_target="tpu_custom_call" | custom-call | tf_op jit(solution)/shard_map/attend/pallas_call | solution.py:441
  15.3 2.1 %collective-permute-start.3 = (bf16[224,128]{1,0:T(8,128)(2,1)S(1)}, bf16[224,128]{1,0:T(8,128)(2,1)S(1)}, u32[]{:S(2)}, u32[]{:S(2)}) collective-permute-start(bf16[224,128]{1,0:T(8,128)(2,1)S(1)} %get-tuple-element.19), channel_id=1, source_target_pairs={{0,12},{4,8},{8,4},{12,0},{1,13},{5,9},{9,5},{13,1},{2,14},{6,10},... | collective-permute-start | bytes 172040 | tf_op jit(solution)/shard_map/ppermute | solution.py:418
  17.4 0.0 collective-permute-start.4
  17.4 2.4 %collective-permute-start.5 = (bf16[224,128]{1,0:T(8,128)(2,1)S(1)}, bf16[224,128]{1,0:T(8,128)(2,1)S(1)}, u32[]{:S(2)}, u32[]{:S(2)}) collective-permute-start(bf16[224,128]{1,0:T(8,128)(2,1)S(1)} %get-tuple-element.21), channel_id=1, source_target_pairs={{0,8},{4,12},{8,0},{12,4},{1,9},{5,13},{9,1},{13,5},{2,10},{6,14},... | collective-permute-start | bytes 172040 | tf_op jit(solution)/shard_map/ppermute | solution.py:418
  19.7 2.1 %collective-permute-done.3.refs_1_ = bf16[224,128]{1,0:T(8,128)(2,1)S(1)} collective-permute-done((bf16[224,128]{1,0:T(8,128)(2,1)S(1)}, bf16[224,128]{1,0:T(8,128)(2,1)S(1)}, u32[]{:S(2)}, u32[]{:S(2)}) %collective-permute-start.3) | collective-permute-done | bytes 57376 | tf_op jit(solution)/shard_map/ppermute | solution.py:418
  21.9 0.8 %collective-permute-done.4.refs_2_ = bf16[224,128]{1,0:T(8,128)(2,1)S(1)} collective-permute-done((bf16[224,128]{1,0:T(8,128)(2,1)S(1)}, bf16[224,128]{1,0:T(8,128)(2,1)S(1)}, u32[]{:S(2)}, u32[]{:S(2)}) %collective-permute-start.4) | collective-permute-done | bytes 57376 | tf_op jit(solution)/shard_map/ppermute | solution.py:418
  22.7 0.0 collective-permute-done.5.refs_3_
  22.7 0.8 %combine.1 = (bf16[2,32,128]{2,1,0:T(8,128)(2,1)}, bf16[2,16,576]{2,1,0:T(8,128)(2,1)}) custom-call(bf16[224,128]{1,0:T(8,128)(2,1)S(1)} %get-tuple-element.18.refs_0_, bf16[224,128]{1,0:T(8,128)(2,1)S(1)} %collective-permute-done.3.refs_1_, bf16[224,128]{1,0:T(8,128)(2,1)S(1)} %collective-permute-done.4.refs_2_, ...), custom_call_target="tpu_custom_call" | custom-call | tf_op jit(solution)/shard_map/combine/pallas_call | solution.py:468
Async XLA Ops:
  1.7 8.5 %collective-permute-start.2 = (bf16[160,128]{1,0:T(8,128)(2,1)S(1)}, bf16[160,128]{1,0:T(8,128)(2,1)S(1)}, u32[]{:S(2)}, u32[]{:S(2)}) collective-permute-start(bf16[160,128]{1,0:T(8,128)(2,1)S(1)} %get-tuple-element.12.refs_0_), channel_id=1, source_target_pairs={{0,8},{4,12},{8,0},{12,4},{1,9},{5,13},{9,1},{13,5},{2,10},{6,14},... | collective-permute-start | bytes 122888 | tf_op jit(solution)/shard_map/ppermute | solution.py:418
  5.8 5.8 %collective-permute-start.1 = (bf16[160,128]{1,0:T(8,128)(2,1)S(1)}, bf16[160,128]{1,0:T(8,128)(2,1)S(1)}, u32[]{:S(2)}, u32[]{:S(2)}) collective-permute-start(bf16[160,128]{1,0:T(8,128)(2,1)S(1)} %get-tuple-element.12.refs_0_), channel_id=1, source_target_pairs={{0,12},{4,8},{8,4},{12,0},{1,13},{5,9},{9,5},{13,1},{2,14},{6,10},... | collective-permute-start | bytes 122888 | tf_op jit(solution)/shard_map/ppermute | solution.py:418
  7.1 4.5 %collective-permute-start = (bf16[160,128]{1,0:T(8,128)(2,1)S(1)}, bf16[160,128]{1,0:T(8,128)(2,1)S(1)}, u32[]{:S(2)}, u32[]{:S(2)}) collective-permute-start(bf16[160,128]{1,0:T(8,128)(2,1)S(1)} %get-tuple-element.12.refs_0_), channel_id=1, source_target_pairs={{0,4},{4,0},{8,12},{12,8},{1,5},{5,1},{9,13},{13,9},{2,6},{6,2},{1... | collective-permute-start | bytes 122888 | tf_op jit(solution)/shard_map/ppermute | solution.py:418
  15.3 6.6 %collective-permute-start.3 = (bf16[224,128]{1,0:T(8,128)(2,1)S(1)}, bf16[224,128]{1,0:T(8,128)(2,1)S(1)}, u32[]{:S(2)}, u32[]{:S(2)}) collective-permute-start(bf16[224,128]{1,0:T(8,128)(2,1)S(1)} %get-tuple-element.19), channel_id=1, source_target_pairs={{0,12},{4,8},{8,4},{12,0},{1,13},{5,9},{9,5},{13,1},{2,14},{6,10},... | collective-permute-start | bytes 172040 | tf_op jit(solution)/shard_map/ppermute | solution.py:418
  17.4 5.3 %collective-permute-start.4 = (bf16[224,128]{1,0:T(8,128)(2,1)S(1)}, bf16[224,128]{1,0:T(8,128)(2,1)S(1)}, u32[]{:S(2)}, u32[]{:S(2)}) collective-permute-start(bf16[224,128]{1,0:T(8,128)(2,1)S(1)} %get-tuple-element.20), channel_id=1, source_target_pairs={{0,4},{4,0},{8,12},{12,8},{1,5},{5,1},{9,13},{13,9},{2,6},{6,2},{1... | collective-permute-start | bytes 172040 | tf_op jit(solution)/shard_map/ppermute | solution.py:418
  17.4 5.3 %collective-permute-start.5 = (bf16[224,128]{1,0:T(8,128)(2,1)S(1)}, bf16[224,128]{1,0:T(8,128)(2,1)S(1)}, u32[]{:S(2)}, u32[]{:S(2)}) collective-permute-start(bf16[224,128]{1,0:T(8,128)(2,1)S(1)} %get-tuple-element.21), channel_id=1, source_target_pairs={{0,8},{4,12},{8,0},{12,4},{1,9},{5,13},{9,1},{13,5},{2,10},{6,14},... | collective-permute-start | bytes 172040 | tf_op jit(solution)/shard_map/ppermute | solution.py:418

commit v4 on v3

--- a/solution.py
+++ b/solution.py
@@ -188,13 +188,25 @@
         for n in range(each.shape[0]):
             each[n, rows * k : rows * (k + 1), :] = told[rows * n : rows * (n + 1), :]
 
-    def absorb(h):
-        one_head = q_flat[pl.ds(h, everyone, stride=heads), :].astype(BF)
-        absorbed = jnp.dot(one_head, w_uk[h], preferred_element_type=F32)
-        for c in range(tiles):
-            lat[c, pl.ds(h, everyone, stride=heads), :] = absorbed[:, c * LANES : (c + 1) * LANES]
-
-    each_of(heads, ABSORB_UNROLL, absorb)
+    none = jnp.zeros((everyone, LANES), F32)
+
+    def absorb(pair):
+        h = 2 * pair
+        two = [q_flat[pl.ds(h + n, everyone, stride=heads), :] for n in range(2)]
+        two = jnp.concatenate(
+            [jnp.concatenate([two[0], none], axis=1), jnp.concatenate([none, two[1]], axis=1)],
+            axis=0,
+        ).astype(BF)
+        absorbed = jnp.dot(
+            two, w_uk[h : h + 2].reshape(2 * LANES, kvl), preferred_element_type=F32
+        )
+        for n in range(2):
+            for c in range(tiles):
+                lat[c, pl.ds(h + n, everyone, stride=heads), :] = absorbed[
+                    n * everyone : (n + 1) * everyone, c * LANES : (c + 1) * LANES
+                ]
+
+    each_of(heads // 2, ABSORB_UNROLL, absorb)
 
     counts = jnp.concatenate([each[COUNT + w] for w in range(wide)], axis=1).astype(BF)
     counts = jnp.dot(counts, row_place[...], preferred_element_type=F32)
@@ -210,6 +222,56 @@
         full, flat_pool, (((1,), (1,)), ((), ())), preferred_element_type=F32
     )
 
+    new_score = jnp.zeros((queries, LANES), F32)
+    new_c = []
+    for c in range(tiles):
+        new_c.append(
+            jnp.concatenate(
+                [
+                    jnp.broadcast_to(
+                        home[r : r + 1, c * LANES : (c + 1) * LANES], (heads, LANES)
+                    )
+                    for r in range(rows)
+                ],
+                axis=0,
+            )
+        )
+        new_score = new_score + rounded(lat[c, 0:queries, :]) * new_c[c]
+    both = messages[0][queries : 2 * queries, :].astype(F32)
+    both = both + pltpu.roll(both, 64, 1)
+    new_key = jnp.concatenate(
+        [
+            jnp.broadcast_to(home[r : r + 1, kvl : kvl + LANES], (heads, LANES))
+            for r in range(rows)
+        ],
+        axis=0,
+    )
+    new_score = new_score + 0.5 * both * new_key
+    new_score = jnp.sum(new_score, axis=1, keepdims=True) * (SCALE * LOG2E)
+    new_scores[...] = jnp.full(new_scores.shape, NONE, F32)
+    new_scores[0:queries, :] = jnp.broadcast_to(new_score, (queries, LANES))
+
+    chunk = 32
+
+    def soften(n):
+        at = pl.ds(pl.multiple_of(n * chunk, chunk), chunk)
+        if heads >= chunk:
+            shown = bias[pl.ds(n * chunk // heads, 1), :]
+        else:
+            shown = [bias[pl.ds(n * (chunk // heads) + m, 1), :] for m in range(chunk // heads)]
+            shown = [jnp.broadcast_to(one, (heads, tokens)) for one in shown]
+            shown = jnp.concatenate(shown, axis=0)
+        some = scores[at, :] * (SCALE * LOG2E) + shown
+        new = new_scores[at, 0:1]
+        top = jnp.maximum(jnp.max(some, axis=1, keepdims=True), new)
+        weight = jnp.exp2(some - top).astype(BF)
+        weights[at, :] = weight
+        total = jnp.sum(weight.astype(F32), axis=1, keepdims=True)
+        total = jnp.where(top > 0.5 * NONE, total + rounded(jnp.exp2(new - top)), 0.0)
+        tops[at, :] = jnp.broadcast_to(top, (chunk, LANES))
+        totals[at, :] = jnp.broadcast_to(total, (chunk, LANES))
+
+    each_of(owners * queries // chunk, SOFTEN_UNROLL, soften)
     span = block // head_parts
     tails = everyone * span
     reach = near_span(block, head_parts)
@@ -239,56 +301,6 @@
     tail_rows = jnp.dot(chosen, near_pool, preferred_element_type=F32)
     is_new = is_holder & (token == tail_len)
 
-    new_score = jnp.zeros((queries, LANES), F32)
-    new_c = []
-    for c in range(tiles):
-        new_c.append(
-            jnp.concatenate(
-                [
-                    jnp.broadcast_to(
-                        home[r : r + 1, c * LANES : (c + 1) * LANES], (heads, LANES)
-                    )
-                    for r in range(rows)
-                ],
-                axis=0,
-            )
-        )
-        new_score = new_score + rounded(lat[c, 0:queries, :]) * new_c[c]
-    both = messages[0][queries : 2 * queries, :].astype(F32)
-    both = both + pltpu.roll(both, 64, 1)
-    new_key = jnp.concatenate(
-        [
-            jnp.broadcast_to(home[r : r + 1, kvl : kvl + LANES], (heads, LANES))
-            for r in range(rows)
-        ],
-        axis=0,
-    )
-    new_score = new_score + 0.5 * both * new_key
-    new_score = jnp.sum(new_score, axis=1, keepdims=True) * (SCALE * LOG2E)
-    new_scores[...] = jnp.full(new_scores.shape, NONE, F32)
-    new_scores[0:queries, :] = jnp.broadcast_to(new_score, (queries, LANES))
-
-    chunk = 16
-
-    def soften(n):
-        at = pl.ds(pl.multiple_of(n * chunk, chunk), chunk)
-        if heads >= chunk:
-            shown = bias[pl.ds(n * chunk // heads, 1), :]
-        else:
-            shown = [bias[pl.ds(n * (chunk // heads) + m, 1), :] for m in range(chunk // heads)]
-            shown = [jnp.broadcast_to(one, (heads, tokens)) for one in shown]
-            shown = jnp.concatenate(shown, axis=0)
-        some = scores[at, :] * (SCALE * LOG2E) + shown
-        new = new_scores[at, 0:1]
-        top = jnp.maximum(jnp.max(some, axis=1, keepdims=True), new)
-        weight = jnp.exp2(some - top).astype(BF)
-        weights[at, :] = weight
-        total = jnp.sum(weight.astype(F32), axis=1, keepdims=True)
-        total = jnp.where(top > 0.5 * NONE, total + rounded(jnp.exp2(new - top)), 0.0)
-        tops[at, :] = jnp.broadcast_to(top, (chunk, LANES))
-        totals[at, :] = jnp.broadcast_to(total, (chunk, LANES))
-
-    each_of(owners * queries // chunk, SOFTEN_UNROLL, soften)
     sums = jnp.dot(weights[...], flat_pool[:, :kvl], preferred_element_type=F32)
     share = jnp.where(totals[...] > 0.0, 1.0 / jnp.maximum(totals[...], 1e-30), 0.0)
     new_weight = rounded(jnp.exp2(new_scores[0:queries, :] - tops[0:queries, :]))
@@ -301,14 +313,24 @@
         copy.wait()
 
     def project(h):
-        one_head = jnp.concatenate(
-            [lat[c, pl.ds(h, everyone, stride=heads), :] for c in range(tiles)], axis=1
+        two = jnp.concatenate(
+            [
+                jnp.concatenate(
+                    [lat[c, pl.ds(2 * h + n, everyone, stride=heads), :] for c in range(tiles)], axis=1
+                )
+                for n in range(2)
+            ],
+            axis=0,
         ).astype(BF)
-        out[pl.ds(h, everyone, stride=heads), :] = jnp.dot(
-            one_head, w_uv[h], preferred_element_type=F32
+        both = jnp.dot(
+            two, jnp.concatenate([w_uv[2 * h], w_uv[2 * h + 1]], axis=1), preferred_element_type=F32
         )
-
-    each_of(heads, PROJECT_UNROLL, project)
+        for n in range(2):
+            out[pl.ds(2 * h + n, everyone, stride=heads), :] = both[
+                n * everyone : (n + 1) * everyone, n * LANES : (n + 1) * LANES
+            ]
+
+    each_of(heads // 2, PROJECT_UNROLL, project)
 
     lane = lane_ids((heads, LANES))
     tail_lane = lane_ids((rows * span, LANES))

time: 23.6 us -> 23.5 us (level)
  no operation moved by 1% of the time
where the time goes in v4:
time: 23.5 us; the launch traced here: 23.4 us
  starting transfers between devices  10.1 us (43%)
  Pallas kernels  8.26 us (35%)
  waiting for transfers between devices  4.3 us (18%)
  between operations  0.67 us (3%)
    ppermute x6, starting transfers between devices, swap(): return lax.ppermute(array, 'pool', [(i, i ^ k) for i in range(owners)])  10.1 us
    ppermute x6, waiting for transfers between devices, swap(): return lax.ppermute(array, 'pool', [(i, i ^ k) for i in range(owners)])  4.3 us
    pallas_call x1, Pallas kernels, per_device(): pl.pallas_call(functools.partial(attend_kernel, owners, parts, rows, head...  3.59 us
    pallas_call x1, Pallas kernels, per_device(): pl.pallas_call(functools.partial(load_kernel, parts), out_shape=tuple((pl...  2.84 us
    pallas_call x1, Pallas kernels, per_device(): pl.pallas_call(functools.partial(query_kernel, wide), out_shape=(pltpu.VM...  1.01 us
    pallas_call x1, Pallas kernels, per_device(): pl.pallas_call(functools.partial(combine_kernel, rows, heads, span), out_...  0.82 us
  transfers between devices with their start and end apart: 6, of which 3 were waited for; matrix products, arithmetic and copies ran while one was open for 0% of the time, Pallas kernels for 12%

profile of v4, /device:TPU:0, one launch (start us, length us, event | category | flops | bytes accessed | tf_op | source)
XLA Modules:
  0.0 23.4 jit_solution(3235687022111742459)
XLA Ops:
  0.6 1.0 %queries.1 = (bf16[160,128]{1,0:T(8,128)(2,1)S(1)}, f32[8,640]{1,0:T(8,128)S(1)}) custom-call(s32[2,32]{1,0:T(2,128)} %refs_0_.1, s32[2]{0:T(128)} %refs_1_.1, s32[2]{0:T(128)} %refs_2_.1, bf16[2,32,128]{2,1,0:T(8,128)(2,1)} %refs_3_.1, bf16[2,32,64]{2,1,0:T(8,128)(2,1)} %refs_4_.1, bf16[2,576]{1,0:T(2,128)(2,1)} %refs_5_.1, bf16[4,128]{1,0:T(4,128)(2,1)} %bitcast.1, ...), custom_call_target="tpu_custom_call" | custom-call | tf_op jit(solution)/shard_map/queries/pallas_call | solution.py:423
  1.7 4.1 %collective-permute-start.2 = (bf16[160,128]{1,0:T(8,128)(2,1)S(1)}, bf16[160,128]{1,0:T(8,128)(2,1)S(1)}, u32[]{:S(2)}, u32[]{:S(2)}) collective-permute-start(bf16[160,128]{1,0:T(8,128)(2,1)S(1)} %get-tuple-element.12.refs_0_), channel_id=1, source_target_pairs={{0,8},{4,12},{8,0},{12,4},{1,9},{5,13},{9,1},{13,5},{2,10},{6,14},... | collective-permute-start | bytes 122888 | tf_op jit(solution)/shard_map/ppermute | solution.py:440
  5.8 1.3 %collective-permute-start.1 = (bf16[160,128]{1,0:T(8,128)(2,1)S(1)}, bf16[160,128]{1,0:T(8,128)(2,1)S(1)}, u32[]{:S(2)}, u32[]{:S(2)}) collective-permute-start(bf16[160,128]{1,0:T(8,128)(2,1)S(1)} %get-tuple-element.12.refs_0_), channel_id=1, source_target_pairs={{0,12},{4,8},{8,4},{12,0},{1,13},{5,9},{9,5},{13,1},{2,14},{6,10},... | collective-permute-start | bytes 122888 | tf_op jit(solution)/shard_map/ppermute | solution.py:440
  7.1 0.2 collective-permute-start
  7.3 2.8 %load.1 = (bf16[32,128,512]{2,1,0:T(8,128)(2,1)S(1)}, bf16[24,64,640]{2,1,0:T(8,128)(2,1)S(1)}, bf16[128,1536]{1,0:T(8,128)(2,1)S(1)}, bf16[128,512]{1,0:T(8,128)(2,1)S(1)}) custom-call(bf16[32,128,512]{2,1,0:T(8,128)(2,1)} %w_uk_hbm.1, bf16[24,64,576]{2,1,0:T(8,128)(2,1)} %pool_hbm.1), custom_call_target="tpu_custom_call" | custom-call | bytes 20971520 | tf_op jit(solution)/shard_map/load/pallas_call | solution.py:451
  10.2 0.0 collective-permute-done.2.refs_3_
  10.2 1.4 %collective-permute-done.1.refs_2_ = bf16[160,128]{1,0:T(8,128)(2,1)S(1)} collective-permute-done((bf16[160,128]{1,0:T(8,128)(2,1)S(1)}, bf16[160,128]{1,0:T(8,128)(2,1)S(1)}, u32[]{:S(2)}, u32[]{:S(2)}) %collective-permute-start.1) | collective-permute-done | bytes 40992 | tf_op jit(solution)/shard_map/ppermute | solution.py:440
  11.6 0.0 collective-permute-done.refs_1_
  11.6 3.6 %attend.1 = (bf16[224,128]{1,0:T(8,128)(2,1)S(1)}, bf16[224,128]{1,0:T(8,128)(2,1)S(1)}, bf16[224,128]{1,0:T(8,128)(2,1)S(1)}, bf16[224,128]{1,0:T(8,128)(2,1)S(1)}) custom-call(bf16[160,128]{1,0:T(8,128)(2,1)S(1)} %get-tuple-element.12.refs_0_, bf16[160,128]{1,0:T(8,128)(2,1)S(1)} %collective-permute-done.refs_1_, ...), custom_call_target="tpu_custom_call" | custom-call | tf_op jit(solution)/shard_map/attend/pallas_call | solution.py:463
  15.2 2.1 %collective-permute-start.3 = (bf16[224,128]{1,0:T(8,128)(2,1)S(1)}, bf16[224,128]{1,0:T(8,128)(2,1)S(1)}, u32[]{:S(2)}, u32[]{:S(2)}) collective-permute-start(bf16[224,128]{1,0:T(8,128)(2,1)S(1)} %get-tuple-element.19), channel_id=1, source_target_pairs={{0,12},{4,8},{8,4},{12,0},{1,13},{5,9},{9,5},{13,1},{2,14},{6,10},... | collective-permute-start | bytes 172040 | tf_op jit(solution)/shard_map/ppermute | solution.py:440
  17.2 0.0 collective-permute-start.4
  17.2 2.4 %collective-permute-start.5 = (bf16[224,128]{1,0:T(8,128)(2,1)S(1)}, bf16[224,128]{1,0:T(8,128)(2,1)S(1)}, u32[]{:S(2)}, u32[]{:S(2)}) collective-permute-start(bf16[224,128]{1,0:T(8,128)(2,1)S(1)} %get-tuple-element.21), channel_id=1, source_target_pairs={{0,8},{4,12},{8,0},{12,4},{1,9},{5,13},{9,1},{13,5},{2,10},{6,14},... | collective-permute-start | bytes 172040 | tf_op jit(solution)/shard_map/ppermute | solution.py:440
  19.6 2.2 %collective-permute-done.3.refs_1_ = bf16[224,128]{1,0:T(8,128)(2,1)S(1)} collective-permute-done((bf16[224,128]{1,0:T(8,128)(2,1)S(1)}, bf16[224,128]{1,0:T(8,128)(2,1)S(1)}, u32[]{:S(2)}, u32[]{:S(2)}) %collective-permute-start.3) | collective-permute-done | bytes 57376 | tf_op jit(solution)/shard_map/ppermute | solution.py:440
  21.8 0.8 %collective-permute-done.4.refs_2_ = bf16[224,128]{1,0:T(8,128)(2,1)S(1)} collective-permute-done((bf16[224,128]{1,0:T(8,128)(2,1)S(1)}, bf16[224,128]{1,0:T(8,128)(2,1)S(1)}, u32[]{:S(2)}, u32[]{:S(2)}) %collective-permute-start.4) | collective-permute-done | bytes 57376 | tf_op jit(solution)/shard_map/ppermute | solution.py:440
  22.5 0.0 collective-permute-done.5.refs_3_
  22.5 0.8 %combine.1 = (bf16[2,32,128]{2,1,0:T(8,128)(2,1)}, bf16[2,16,576]{2,1,0:T(8,128)(2,1)}) custom-call(bf16[224,128]{1,0:T(8,128)(2,1)S(1)} %get-tuple-element.18.refs_0_, bf16[224,128]{1,0:T(8,128)(2,1)S(1)} %collective-permute-done.3.refs_1_, bf16[224,128]{1,0:T(8,128)(2,1)S(1)} %collective-permute-done.4.refs_2_, ...), custom_call_target="tpu_custom_call" | custom-call | tf_op jit(solution)/shard_map/combine/pallas_call | solution.py:490
Async XLA Ops:
  1.7 8.5 %collective-permute-start.2 = (bf16[160,128]{1,0:T(8,128)(2,1)S(1)}, bf16[160,128]{1,0:T(8,128)(2,1)S(1)}, u32[]{:S(2)}, u32[]{:S(2)}) collective-permute-start(bf16[160,128]{1,0:T(8,128)(2,1)S(1)} %get-tuple-element.12.refs_0_), channel_id=1, source_target_pairs={{0,8},{4,12},{8,0},{12,4},{1,9},{5,13},{9,1},{13,5},{2,10},{6,14},... | collective-permute-start | bytes 122888 | tf_op jit(solution)/shard_map/ppermute | solution.py:440
  5.8 5.8 %collective-permute-start.1 = (bf16[160,128]{1,0:T(8,128)(2,1)S(1)}, bf16[160,128]{1,0:T(8,128)(2,1)S(1)}, u32[]{:S(2)}, u32[]{:S(2)}) collective-permute-start(bf16[160,128]{1,0:T(8,128)(2,1)S(1)} %get-tuple-element.12.refs_0_), channel_id=1, source_target_pairs={{0,12},{4,8},{8,4},{12,0},{1,13},{5,9},{9,5},{13,1},{2,14},{6,10},... | collective-permute-start | bytes 122888 | tf_op jit(solution)/shard_map/ppermute | solution.py:440
  7.1 4.5 %collective-permute-start = (bf16[160,128]{1,0:T(8,128)(2,1)S(1)}, bf16[160,128]{1,0:T(8,128)(2,1)S(1)}, u32[]{:S(2)}, u32[]{:S(2)}) collective-permute-start(bf16[160,128]{1,0:T(8,128)(2,1)S(1)} %get-tuple-element.12.refs_0_), channel_id=1, source_target_pairs={{0,4},{4,0},{8,12},{12,8},{1,5},{5,1},{9,13},{13,9},{2,6},{6,2},{1... | collective-permute-start | bytes 122888 | tf_op jit(solution)/shard_map/ppermute | solution.py:440
  15.2 6.6 %collective-permute-start.3 = (bf16[224,128]{1,0:T(8,128)(2,1)S(1)}, bf16[224,128]{1,0:T(8,128)(2,1)S(1)}, u32[]{:S(2)}, u32[]{:S(2)}) collective-permute-start(bf16[224,128]{1,0:T(8,128)(2,1)S(1)} %get-tuple-element.19), channel_id=1, source_target_pairs={{0,12},{4,8},{8,4},{12,0},{1,13},{5,9},{9,5},{13,1},{2,14},{6,10},... | collective-permute-start | bytes 172040 | tf_op jit(solution)/shard_map/ppermute | solution.py:440
  17.2 5.3 %collective-permute-start.4 = (bf16[224,128]{1,0:T(8,128)(2,1)S(1)}, bf16[224,128]{1,0:T(8,128)(2,1)S(1)}, u32[]{:S(2)}, u32[]{:S(2)}) collective-permute-start(bf16[224,128]{1,0:T(8,128)(2,1)S(1)} %get-tuple-element.20), channel_id=1, source_target_pairs={{0,4},{4,0},{8,12},{12,8},{1,5},{5,1},{9,13},{13,9},{2,6},{6,2},{1... | collective-permute-start | bytes 172040 | tf_op jit(solution)/shard_map/ppermute | solution.py:440
  17.2 5.3 %collective-permute-start.5 = (bf16[224,128]{1,0:T(8,128)(2,1)S(1)}, bf16[224,128]{1,0:T(8,128)(2,1)S(1)}, u32[]{:S(2)}, u32[]{:S(2)}) collective-permute-start(bf16[224,128]{1,0:T(8,128)(2,1)S(1)} %get-tuple-element.21), channel_id=1, source_target_pairs={{0,8},{4,12},{8,0},{12,4},{1,9},{5,13},{9,1},{13,5},{2,10},{6,14},... | collective-permute-start | bytes 172040 | tf_op jit(solution)/shard_map/ppermute | solution.py:440

commit v5 on v4

--- a/solution.py
+++ b/solution.py
@@ -264,9 +264,9 @@
         some = scores[at, :] * (SCALE * LOG2E) + shown
         new = new_scores[at, 0:1]
         top = jnp.maximum(jnp.max(some, axis=1, keepdims=True), new)
-        weight = jnp.exp2(some - top).astype(BF)
-        weights[at, :] = weight
-        total = jnp.sum(weight.astype(F32), axis=1, keepdims=True)
+        weight = jnp.exp2(some - top)
+        weights[at, :] = weight.astype(BF)
+        total = jnp.sum(weight, axis=1, keepdims=True)
         total = jnp.where(top > 0.5 * NONE, total + rounded(jnp.exp2(new - top)), 0.0)
         tops[at, :] = jnp.broadcast_to(top, (chunk, LANES))
         totals[at, :] = jnp.broadcast_to(total, (chunk, LANES))

time: 23.5 us -> 23.5 us (level)
  no operation moved by 1% of the time
where the time goes in v5:
time: 23.5 us; the launch traced here: 23.3 us
  starting transfers between devices  10.1 us (43%)
  Pallas kernels  8.22 us (35%)
  waiting for transfers between devices  4.3 us (18%)
  between operations  0.67 us (3%)
    ppermute x6, starting transfers between devices, swap(): return lax.ppermute(array, 'pool', [(i, i ^ k) for i in range(owners)])  10.1 us
    ppermute x6, waiting for transfers between devices, swap(): return lax.ppermute(array, 'pool', [(i, i ^ k) for i in range(owners)])  4.3 us
    pallas_call x1, Pallas kernels, per_device(): pl.pallas_call(functools.partial(attend_kernel, owners, parts, rows, head...  3.55 us
    pallas_call x1, Pallas kernels, per_device(): pl.pallas_call(functools.partial(load_kernel, parts), out_shape=tuple((pl...  2.84 us
    pallas_call x1, Pallas kernels, per_device(): pl.pallas_call(functools.partial(query_kernel, wide), out_shape=(pltpu.VM...  1.01 us
    pallas_call x1, Pallas kernels, per_device(): pl.pallas_call(functools.partial(combine_kernel, rows, heads, span), out_...  0.82 us
  transfers between devices with their start and end apart: 6, of which 3 were waited for; matrix products, arithmetic and copies ran while one was open for 0% of the time, Pallas kernels for 12%

profile of v5, /device:TPU:0, one launch (start us, length us, event | category | flops | bytes accessed | tf_op | source)
XLA Modules:
  0.0 23.3 jit_solution(7872208741731389243)
XLA Ops:
  0.6 1.0 %queries.1 = (bf16[160,128]{1,0:T(8,128)(2,1)S(1)}, f32[8,640]{1,0:T(8,128)S(1)}) custom-call(s32[2,32]{1,0:T(2,128)} %refs_0_.1, s32[2]{0:T(128)} %refs_1_.1, s32[2]{0:T(128)} %refs_2_.1, bf16[2,32,128]{2,1,0:T(8,128)(2,1)} %refs_3_.1, bf16[2,32,64]{2,1,0:T(8,128)(2,1)} %refs_4_.1, bf16[2,576]{1,0:T(2,128)(2,1)} %refs_5_.1, bf16[4,128]{1,0:T(4,128)(2,1)} %bitcast.1, ...), custom_call_target="tpu_custom_call" | custom-call | tf_op jit(solution)/shard_map/queries/pallas_call | solution.py:423
  1.7 4.1 %collective-permute-start.2 = (bf16[160,128]{1,0:T(8,128)(2,1)S(1)}, bf16[160,128]{1,0:T(8,128)(2,1)S(1)}, u32[]{:S(2)}, u32[]{:S(2)}) collective-permute-start(bf16[160,128]{1,0:T(8,128)(2,1)S(1)} %get-tuple-element.12.refs_0_), channel_id=1, source_target_pairs={{0,8},{4,12},{8,0},{12,4},{1,9},{5,13},{9,1},{13,5},{2,10},{6,14},... | collective-permute-start | bytes 122888 | tf_op jit(solution)/shard_map/ppermute | solution.py:440
  5.8 1.3 %collective-permute-start.1 = (bf16[160,128]{1,0:T(8,128)(2,1)S(1)}, bf16[160,128]{1,0:T(8,128)(2,1)S(1)}, u32[]{:S(2)}, u32[]{:S(2)}) collective-permute-start(bf16[160,128]{1,0:T(8,128)(2,1)S(1)} %get-tuple-element.12.refs_0_), channel_id=1, source_target_pairs={{0,12},{4,8},{8,4},{12,0},{1,13},{5,9},{9,5},{13,1},{2,14},{6,10},... | collective-permute-start | bytes 122888 | tf_op jit(solution)/shard_map/ppermute | solution.py:440
  7.1 0.2 collective-permute-start
  7.3 2.8 %load.1 = (bf16[32,128,512]{2,1,0:T(8,128)(2,1)S(1)}, bf16[24,64,640]{2,1,0:T(8,128)(2,1)S(1)}, bf16[128,1536]{1,0:T(8,128)(2,1)S(1)}, bf16[128,512]{1,0:T(8,128)(2,1)S(1)}) custom-call(bf16[32,128,512]{2,1,0:T(8,128)(2,1)} %w_uk_hbm.1, bf16[24,64,576]{2,1,0:T(8,128)(2,1)} %pool_hbm.1), custom_call_target="tpu_custom_call" | custom-call | bytes 20971520 | tf_op jit(solution)/shard_map/load/pallas_call | solution.py:451
  10.2 0.0 collective-permute-done.2.refs_3_
  10.2 1.4 %collective-permute-done.1.refs_2_ = bf16[160,128]{1,0:T(8,128)(2,1)S(1)} collective-permute-done((bf16[160,128]{1,0:T(8,128)(2,1)S(1)}, bf16[160,128]{1,0:T(8,128)(2,1)S(1)}, u32[]{:S(2)}, u32[]{:S(2)}) %collective-permute-start.1) | collective-permute-done | bytes 40992 | tf_op jit(solution)/shard_map/ppermute | solution.py:440
  11.6 0.0 collective-permute-done.refs_1_
  11.6 3.6 %attend.1 = (bf16[224,128]{1,0:T(8,128)(2,1)S(1)}, bf16[224,128]{1,0:T(8,128)(2,1)S(1)}, bf16[224,128]{1,0:T(8,128)(2,1)S(1)}, bf16[224,128]{1,0:T(8,128)(2,1)S(1)}) custom-call(bf16[160,128]{1,0:T(8,128)(2,1)S(1)} %get-tuple-element.12.refs_0_, bf16[160,128]{1,0:T(8,128)(2,1)S(1)} %collective-permute-done.refs_1_, ...), custom_call_target="tpu_custom_call" | custom-call | tf_op jit(solution)/shard_map/attend/pallas_call | solution.py:463
  15.1 2.1 %collective-permute-start.3 = (bf16[224,128]{1,0:T(8,128)(2,1)S(1)}, bf16[224,128]{1,0:T(8,128)(2,1)S(1)}, u32[]{:S(2)}, u32[]{:S(2)}) collective-permute-start(bf16[224,128]{1,0:T(8,128)(2,1)S(1)} %get-tuple-element.19), channel_id=1, source_target_pairs={{0,12},{4,8},{8,4},{12,0},{1,13},{5,9},{9,5},{13,1},{2,14},{6,10},... | collective-permute-start | bytes 172040 | tf_op jit(solution)/shard_map/ppermute | solution.py:440
  17.2 0.0 collective-permute-start.4
  17.2 2.4 %collective-permute-start.5 = (bf16[224,128]{1,0:T(8,128)(2,1)S(1)}, bf16[224,128]{1,0:T(8,128)(2,1)S(1)}, u32[]{:S(2)}, u32[]{:S(2)}) collective-permute-start(bf16[224,128]{1,0:T(8,128)(2,1)S(1)} %get-tuple-element.21), channel_id=1, source_target_pairs={{0,8},{4,12},{8,0},{12,4},{1,9},{5,13},{9,1},{13,5},{2,10},{6,14},... | collective-permute-start | bytes 172040 | tf_op jit(solution)/shard_map/ppermute | solution.py:440
  19.6 2.1 %collective-permute-done.3.refs_1_ = bf16[224,128]{1,0:T(8,128)(2,1)S(1)} collective-permute-done((bf16[224,128]{1,0:T(8,128)(2,1)S(1)}, bf16[224,128]{1,0:T(8,128)(2,1)S(1)}, u32[]{:S(2)}, u32[]{:S(2)}) %collective-permute-start.3) | collective-permute-done | bytes 57376 | tf_op jit(solution)/shard_map/ppermute | solution.py:440
  21.7 0.8 %collective-permute-done.4.refs_2_ = bf16[224,128]{1,0:T(8,128)(2,1)S(1)} collective-permute-done((bf16[224,128]{1,0:T(8,128)(2,1)S(1)}, bf16[224,128]{1,0:T(8,128)(2,1)S(1)}, u32[]{:S(2)}, u32[]{:S(2)}) %collective-permute-start.4) | collective-permute-done | bytes 57376 | tf_op jit(solution)/shard_map/ppermute | solution.py:440
  22.5 0.0 collective-permute-done.5.refs_3_
  22.5 0.8 %combine.1 = (bf16[2,32,128]{2,1,0:T(8,128)(2,1)}, bf16[2,16,576]{2,1,0:T(8,128)(2,1)}) custom-call(bf16[224,128]{1,0:T(8,128)(2,1)S(1)} %get-tuple-element.18.refs_0_, bf16[224,128]{1,0:T(8,128)(2,1)S(1)} %collective-permute-done.3.refs_1_, bf16[224,128]{1,0:T(8,128)(2,1)S(1)} %collective-permute-done.4.refs_2_, ...), custom_call_target="tpu_custom_call" | custom-call | tf_op jit(solution)/shard_map/combine/pallas_call | solution.py:490
Async XLA Ops:
  1.7 8.5 %collective-permute-start.2 = (bf16[160,128]{1,0:T(8,128)(2,1)S(1)}, bf16[160,128]{1,0:T(8,128)(2,1)S(1)}, u32[]{:S(2)}, u32[]{:S(2)}) collective-permute-start(bf16[160,128]{1,0:T(8,128)(2,1)S(1)} %get-tuple-element.12.refs_0_), channel_id=1, source_target_pairs={{0,8},{4,12},{8,0},{12,4},{1,9},{5,13},{9,1},{13,5},{2,10},{6,14},... | collective-permute-start | bytes 122888 | tf_op jit(solution)/shard_map/ppermute | solution.py:440
  5.8 5.8 %collective-permute-start.1 = (bf16[160,128]{1,0:T(8,128)(2,1)S(1)}, bf16[160,128]{1,0:T(8,128)(2,1)S(1)}, u32[]{:S(2)}, u32[]{:S(2)}) collective-permute-start(bf16[160,128]{1,0:T(8,128)(2,1)S(1)} %get-tuple-element.12.refs_0_), channel_id=1, source_target_pairs={{0,12},{4,8},{8,4},{12,0},{1,13},{5,9},{9,5},{13,1},{2,14},{6,10},... | collective-permute-start | bytes 122888 | tf_op jit(solution)/shard_map/ppermute | solution.py:440
  7.1 4.5 %collective-permute-start = (bf16[160,128]{1,0:T(8,128)(2,1)S(1)}, bf16[160,128]{1,0:T(8,128)(2,1)S(1)}, u32[]{:S(2)}, u32[]{:S(2)}) collective-permute-start(bf16[160,128]{1,0:T(8,128)(2,1)S(1)} %get-tuple-element.12.refs_0_), channel_id=1, source_target_pairs={{0,4},{4,0},{8,12},{12,8},{1,5},{5,1},{9,13},{13,9},{2,6},{6,2},{1... | collective-permute-start | bytes 122888 | tf_op jit(solution)/shard_map/ppermute | solution.py:440
  15.1 6.6 %collective-permute-start.3 = (bf16[224,128]{1,0:T(8,128)(2,1)S(1)}, bf16[224,128]{1,0:T(8,128)(2,1)S(1)}, u32[]{:S(2)}, u32[]{:S(2)}) collective-permute-start(bf16[224,128]{1,0:T(8,128)(2,1)S(1)} %get-tuple-element.19), channel_id=1, source_target_pairs={{0,12},{4,8},{8,4},{12,0},{1,13},{5,9},{9,5},{13,1},{2,14},{6,10},... | collective-permute-start | bytes 172040 | tf_op jit(solution)/shard_map/ppermute | solution.py:440
  17.2 5.3 %collective-permute-start.4 = (bf16[224,128]{1,0:T(8,128)(2,1)S(1)}, bf16[224,128]{1,0:T(8,128)(2,1)S(1)}, u32[]{:S(2)}, u32[]{:S(2)}) collective-permute-start(bf16[224,128]{1,0:T(8,128)(2,1)S(1)} %get-tuple-element.20), channel_id=1, source_target_pairs={{0,4},{4,0},{8,12},{12,8},{1,5},{5,1},{9,13},{13,9},{2,6},{6,2},{1... | collective-permute-start | bytes 172040 | tf_op jit(solution)/shard_map/ppermute | solution.py:440
  17.2 5.3 %collective-permute-start.5 = (bf16[224,128]{1,0:T(8,128)(2,1)S(1)}, bf16[224,128]{1,0:T(8,128)(2,1)S(1)}, u32[]{:S(2)}, u32[]{:S(2)}) collective-permute-start(bf16[224,128]{1,0:T(8,128)(2,1)S(1)} %get-tuple-element.21), channel_id=1, source_target_pairs={{0,8},{4,12},{8,0},{12,4},{1,9},{5,13},{9,1},{13,5},{2,10},{6,14},... | collective-permute-start | bytes 172040 | tf_op jit(solution)/shard_map/ppermute | solution.py:440
